TPU v7x, 256 devices: a whole 4x4x8 slice. The times are simulated.
256 devices in a mesh: dp: 4 (over y), expert: 64 (over z, x, core).
Axes of the slice: x: 4, y: 4, z: 8, core: 2. Of those that a mesh axis runs over, the one named last changes fastest.
Arguments:
- tokens: bfloat16 [32768, 2048], P(('dp', 'expert')), may hold values from -6 to 6
- cotangent: bfloat16 [32768, 2048], P(('dp', 'expert')), may hold values from -0.3984375 to 0.3984375
- routing: int32 [32768, 8], P(('dp', 'expert')), may hold values from 0 to 31, as said below
- router_route_weights: float32 [32768, 8], P(('dp', 'expert')), may hold values from 0.1 to 1
- route_replica_choice: int32 [32768, 8], P(('dp', 'expert')), may hold values from 0 to 11
- device_expert_table: int32 [64], replicated, may hold values from 0 to 31, as said below
- gate_up_weight: bfloat16 [64, 2048, 1536], P('expert'), may hold values from -1 to 1, as said below
- down_weight: bfloat16 [64, 768, 2048], P('expert'), may hold values from -1 to 1, as said below
- adapter_down_maps: bfloat16 [64, 2048, 128], P('expert'), may hold values from -1 to 1, as said below
- adapter_up_maps: bfloat16 [64, 2, 64, 768], P('expert'), may hold values from -2 to 2, as said below
Outputs:
- mixed: bfloat16 [32768, 2048], P(('dp', 'expert'))
- grad_a: float32 [64, 2048, 128], P('expert')
- grad_b: float32 [64, 2, 64, 768], P('expert')
Inputs may be any that keep to these rules, and one draw needn't show every extreme that they name: `routing`: each row names 8 different experts; experts held by more entries of device_expert_table are chosen more often. `device_expert_table`: every expert of 0 to 31 is held by one to four entries. `gate_up_weight`: entries of device_expert_table that are equal hold equal matrices. `down_weight`: entries of device_expert_table that are equal hold equal matrices. `adapter_down_maps`: entries of device_expert_table that are equal hold equal matrices. `adapter_up_maps`: entries of device_expert_table that are equal hold equal matrices.
All inputs are finite; a program needn't handle non-finite values.
Results may differ from a plain program's by a relative error of at most 0.006.
Values may be sent and summed in bfloat16 or wider, within the bound.
A program may use at most 128 MiB of HBM per device.

v0:
```python
import jax
import jax.numpy as jnp
from jax import lax
from jax.sharding import PartitionSpec as P

ADAPTER_SCALE = 0.5


def route_rows(routing, route_replica_choice, device_expert_table, capacity):
    slot_total = device_expert_table.shape[0]
    route_total = routing.shape[0] * routing.shape[1]
    expert_flat = routing.reshape(-1)
    holds_mask = (expert_flat[:, None] == device_expert_table[None, :]).astype(jnp.int32)
    copies = jnp.sum(holds_mask, axis=1)
    wanted = route_replica_choice.reshape(-1) % copies
    before = jnp.cumsum(holds_mask, axis=1) - holds_mask
    picked = holds_mask * (before == wanted[:, None]).astype(jnp.int32)
    ahead_of = jnp.cumsum(picked, axis=0) - picked
    position = jnp.sum(picked * ahead_of, axis=1)
    target = jnp.sum(picked * jnp.arange(slot_total, dtype=jnp.int32)[None, :], axis=1)
    kept_mask = position < capacity
    dest_index = jnp.where(kept_mask, target * capacity + position, slot_total * capacity)
    source = jnp.full((slot_total * capacity,), route_total, jnp.int32)
    source = source.at[dest_index].set(jnp.arange(route_total, dtype=jnp.int32), mode="drop")
    return (kept_mask, dest_index, source)


def expert_apply_forward(rows_in, gate_up, down, adapt_a, adapt_b):
    adapter_rank_count = adapt_b.shape[1]
    hidden_width = adapt_b.shape[2]
    reduced_rank_rows = jnp.dot(rows_in, adapt_a, preferred_element_type=jnp.float32).astype(
        jnp.bfloat16
    )
    base_preactivation = jnp.dot(rows_in, gate_up, preferred_element_type=jnp.float32)
    adapter_gate_delta = jnp.dot(
        reduced_rank_rows[:, :adapter_rank_count], adapt_b[0], preferred_element_type=jnp.float32
    )
    adapter_up_delta = jnp.dot(
        reduced_rank_rows[:, adapter_rank_count:], adapt_b[1], preferred_element_type=jnp.float32
    )
    gate_preactivation = base_preactivation[:, :hidden_width] + ADAPTER_SCALE * adapter_gate_delta
    up_preactivation = base_preactivation[:, hidden_width:] + ADAPTER_SCALE * adapter_up_delta
    sigmoid_gate = jax.nn.sigmoid(gate_preactivation)
    active = gate_preactivation * sigmoid_gate
    hidden = (active * up_preactivation).astype(jnp.bfloat16)
    layer_output = jnp.dot(hidden, down, preferred_element_type=jnp.float32).astype(jnp.bfloat16)
    return (
        layer_output,
        (reduced_rank_rows, gate_preactivation, up_preactivation, sigmoid_gate, active),
    )


def expert_backward(rows_in, scaled, down, adapt_b, saved_residuals):
    reduced_rank_rows, gate_preactivation, up_preactivation, sigmoid_gate, active = saved_residuals
    adapter_rank_count = adapt_b.shape[1]
    back_hidden = lax.dot_general(
        scaled, down, (((1,), (1,)), ((), ())), preferred_element_type=jnp.float32
    )
    up_preactivation_gradient = (back_hidden * active).astype(jnp.bfloat16)
    slope = sigmoid_gate * (1.0 + gate_preactivation * (1.0 - sigmoid_gate))
    gate_preactivation_gradient = (back_hidden * up_preactivation * slope).astype(jnp.bfloat16)
    row_dimension_numbers = (((0,), (0,)), ((), ()))
    gate_up_map_gradient = ADAPTER_SCALE * lax.dot_general(
        reduced_rank_rows[:, :adapter_rank_count],
        gate_preactivation_gradient,
        row_dimension_numbers,
        preferred_element_type=jnp.float32,
    )
    up_map_gradient = ADAPTER_SCALE * lax.dot_general(
        reduced_rank_rows[:, adapter_rank_count:],
        up_preactivation_gradient,
        row_dimension_numbers,
        preferred_element_type=jnp.float32,
    )
    cols_dims = (((1,), (1,)), ((), ()))
    gate_reduced_rows = lax.dot_general(
        gate_preactivation_gradient, adapt_b[0], cols_dims, preferred_element_type=jnp.float32
    )
    up_reduced_rows = lax.dot_general(
        up_preactivation_gradient, adapt_b[1], cols_dims, preferred_element_type=jnp.float32
    )
    reduced_gradient = (
        ADAPTER_SCALE * jnp.concatenate([gate_reduced_rows, up_reduced_rows], axis=1)
    ).astype(jnp.bfloat16)
    grad_adapt_a = lax.dot_general(
        rows_in, reduced_gradient, row_dimension_numbers, preferred_element_type=jnp.float32
    )
    return (grad_adapt_a, jnp.stack([gate_up_map_gradient, up_map_gradient]))


def body(
    tokens,
    cotangent,
    routing,
    router_route_weights,
    route_replica_choice,
    device_expert_table,
    gate_up_weight,
    down_weight,
    adapter_down_maps,
    adapter_up_maps,
):
    slot_total = lax.axis_size("expert")
    tok_rows = tokens.shape[0]
    model_feature_width = tokens.shape[1]
    top_routes = routing.shape[1]
    route_total = tok_rows * top_routes
    capacity = route_total // slot_total
    kept_mask, dest_index, source = route_rows(
        routing, route_replica_choice, device_expert_table, capacity
    )
    valid_route_mask = source < route_total
    safe_route = jnp.minimum(source, route_total - 1)
    route_token_index = safe_route // top_routes
    weight_flat = router_route_weights.reshape(-1)
    route_weight_rows = weight_flat[safe_route]
    zero_row = jnp.zeros((), jnp.bfloat16)
    rows_out = jnp.where(valid_route_mask[:, None], tokens[route_token_index], zero_row).reshape(
        slot_total, capacity, model_feature_width
    )
    product = (
        route_weight_rows[:, None] * cotangent[route_token_index].astype(jnp.float32)
    ).astype(jnp.bfloat16)
    scaled_out = jnp.where(valid_route_mask[:, None], product, zero_row).reshape(
        slot_total, capacity, model_feature_width
    )
    rows_in = lax.all_to_all(rows_out, "expert", split_axis=0, concat_axis=0, tiled=True)
    flattened_rows = rows_in.reshape(-1, model_feature_width)
    layer_output, saved_residuals = expert_apply_forward(
        flattened_rows, gate_up_weight[0], down_weight[0], adapter_down_maps[0], adapter_up_maps[0]
    )
    returned = lax.all_to_all(
        layer_output.reshape(slot_total, capacity, model_feature_width),
        "expert",
        split_axis=0,
        concat_axis=0,
        tiled=True,
    )
    returned = returned.reshape(-1, model_feature_width)
    picked_rows = returned[jnp.minimum(dest_index, slot_total * capacity - 1)]
    weighted = jnp.where(
        kept_mask[:, None],
        weight_flat[:, None] * picked_rows.astype(jnp.float32),
        jnp.zeros((), jnp.float32),
    )
    mixed = jnp.sum(weighted.reshape(tok_rows, top_routes, model_feature_width), axis=1).astype(
        jnp.bfloat16
    )
    scaled_input_rows = lax.all_to_all(
        scaled_out, "expert", split_axis=0, concat_axis=0, tiled=True
    )
    grad_adapt_a, grad_adapt_b = expert_backward(
        flattened_rows,
        scaled_input_rows.reshape(-1, model_feature_width),
        down_weight[0],
        adapter_up_maps[0],
        saved_residuals,
    )
    piece_a = grad_adapt_a.reshape(slot_total, -1)
    piece_b = grad_adapt_b.reshape(slot_total, -1)
    expert_total = max(top_routes, slot_total // 2)
    members = (
        jnp.arange(expert_total, dtype=jnp.int32)[:, None] == device_expert_table[None, :]
    ).astype(jnp.float32)
    piece_a, piece_b = lax.psum((piece_a, piece_b), "dp")
    got_a, got_b = (
        lax.all_to_all(piece_a, "expert", split_axis=0, concat_axis=0, tiled=True),
        lax.all_to_all(piece_b, "expert", split_axis=0, concat_axis=0, tiled=True),
    )
    expert_a = jnp.dot(members, got_a, precision=lax.Precision.HIGHEST)
    expert_b = jnp.dot(members, got_b, precision=lax.Precision.HIGHEST)
    back_dims = (((0,), (0,)), ((), ()))
    spread_a = lax.dot_general(members, expert_a, back_dims, precision=lax.Precision.HIGHEST)
    spread_b = lax.dot_general(members, expert_b, back_dims, precision=lax.Precision.HIGHEST)
    summed_a, summed_b = (
        lax.all_to_all(spread_a, "expert", split_axis=0, concat_axis=0, tiled=True),
        lax.all_to_all(spread_b, "expert", split_axis=0, concat_axis=0, tiled=True),
    )
    grad_a = summed_a.reshape(grad_adapt_a.shape)[None]
    grad_b = summed_b.reshape(grad_adapt_b.shape)[None]
    return (mixed, grad_a, grad_b)


def solution(mesh):
    return jax.shard_map(
        body,
        mesh=mesh,
        in_specs=(
            P(("dp", "expert"), None),
            P(("dp", "expert"), None),
            P(("dp", "expert"), None),
            P(("dp", "expert"), None),
            P(("dp", "expert"), None),
            P(),
            P("expert", None, None),
            P("expert", None, None),
            P("expert", None, None),
            P("expert", None, None, None),
        ),
        out_specs=(
            P(("dp", "expert"), None),
            P("expert", None, None),
            P("expert", None, None, None),
        ),
        check_vma=False,
    )
```

profile of v0, /device:TPU:1, one launch (start us, length us, event | category | flops | bytes accessed | tf_op | source)
XLA Modules:
  0.0 610.8 jit_solution(4256677529806217968)
XLA Ops:
  14.2 34.2 %reduce-window.6 = s32[64,8,128]{2,1,0:T(8,128)} reduce-window(s32[64,8,128]{2,1,0:T(8,128)} %bitcast.88, s32[]{:T(128)} %constant.15.clone.1), window={size=1x1x128 pad=0_0x0_0x127_0}, to_apply=%region_2.3 | reduce-window | flops 8323072 | bytes 524292 | tf_op jit(solution)/shard_map/reduce-window
  48.4 1.8 slice.46
  53.3 4.3 scatter_custom_fusion
  57.9 4.5 gather_fusion.2
  62.5 9.9 %gather_fusion.3 = bf16[1024,2048]{1,0:T(8,128)(2,1)} fusion(bf16[128,2048]{1,0:T(8,128)(2,1)} %param.11, s32[1024]{0:T(1024)S(1)} %get-tuple-element.12), kind=kCustom, calls=%fused_computation.3 | custom fusion | bytes 8392704 | tf_op jit(solution)/shard_map/gather | solution.py:122
  72.4 10.0 %gather_fusion = bf16[1024,2048]{1,0:T(8,128)(2,1)} fusion(bf16[128,2048]{1,0:T(8,128)(2,1)} %param.10, s32[1024]{0:T(1024)S(1)} %get-tuple-element.12), kind=kCustom, calls=%fused_computation | custom fusion | bytes 8392704 | tf_op jit(solution)/shard_map/gather | solution.py:118
  82.4 6.7 %fusion.5 = (bf16[64,16,2048]{2,1,0:T(8,128)(2,1)}, bf16[64,16,2048]{2,1,0:T(8,128)(2,1)S(1)}) fusion(bf16[64,16,2048]{2,1,0:T(8,128)(2,1)} %bitcast.83, f32[64,16]{1,0:T(8,128)S(1)} %mul.102, pred[64,16]{1,0:T(8,128)(4,1)S(1)} %broadcast_in_dim.56, bf16[64,16,2048]{2,1,0:T(8,128)(2,1)} %bitcast.84), kind=kLoop, calls=%fused_computation.13 | loop fusion | flops 10485760 | bytes 16782336 | tf_op jit(solution)/shard_map/jit(_where)/select_n | solution.py:124
  89.1 107.5 %all_to_all.58 = bf16[64,16,2048]{2,1,0:T(8,128)(2,1)} all-to-all(bf16[64,16,2048]{2,1,0:T(8,128)(2,1)S(1)} %get-tuple-element.10), channel_id=1, replica_groups=mesh['dp'=4,'expert'=64] {'expert'}, dimensions={0} | all-to-all | bytes 8388608 | tf_op jit(solution)/shard_map/all_to_all | solution.py:127
  196.6 7.2 %all-to-all-start.2 = ((bf16[64,16,2048]{2,1,0:T(8,128)(2,1)}), bf16[64,16,2048]{2,1,0:T(8,128)(2,1)}, u32[]{:S(2)}, u32[]{:S(2)}) async-start(bf16[64,16,2048]{2,1,0:T(8,128)(2,1)} %get-tuple-element.9), calls=%async_computation.2 | async-start | bytes 8388608 | tf_op jit(solution)/shard_map/all_to_all | solution.py:149
  204.1 4.0 convolution_convert_fusion.1
  208.0 10.5 %fusion.3 = f32[1024,1536]{1,0:T(8,128)} fusion(bf16[1024,2048]{1,0:T(8,128)(2,1)S(1)} %bitcast.82, bf16[1,2048,1536]{2,1,0:T(8,128)(2,1)} %param.16), kind=kOutput, calls=%fused_computation.10 | convolution fusion | flops 6442450944 | bytes 16777216 | tf_op jit(solution)/shard_map/dot_general | solution.py:34
  218.6 79.8 %all-to-all-done.2 = bf16[64,16,2048]{2,1,0:T(8,128)(2,1)} async-done(((bf16[64,16,2048]{2,1,0:T(8,128)(2,1)}), bf16[64,16,2048]{2,1,0:T(8,128)(2,1)}, u32[]{:S(2)}, u32[]{:S(2)}) %all-to-all-start.2) | async-done | bytes 4194336 | tf_op jit(solution)/shard_map/all_to_all | solution.py:149
  298.4 5.4 fusion.6
  304.4 3.1 multiply_convert_fusion.1
  312.1 4.5 fusion.27
  316.7 52.0 %all-reduce.3.cloned.1.call-done = (f32[64,1,4096]{2,1,0:T(1,128)}, f32[64,1,1536]{2,1,0:T(1,128)}) async-done(((f32[64,1,4096]{2,1,0:T(1,128)}, f32[64,1,1536]{2,1,0:T(1,128)}), (f32[64,1,4096]{2,1,0:T(1,128)}, f32[64,1,1536]{2,1,0:T(1,128)})) %all-reduce.3.cloned.1.call-update) | async-done | bytes 1441808 | tf_op jit(solution)/shard_map/psum | solution.py:165
  368.7 25.9 %all_to_all.59 = f32[64,1,1536]{2,1,0:T(1,128)S(1)} all-to-all(f32[64,1,1536]{2,1,0:T(1,128)} %get-tuple-element.6), channel_id=1, replica_groups=mesh['dp'=4,'expert'=64] {'expert'}, dimensions={0} | all-to-all | bytes 786432 | tf_op jit(solution)/shard_map/all_to_all | solution.py:168
  394.6 5.8 all-to-all-start.3
  402.2 26.1 %all-to-all-done.3 = f32[64,1,4096]{2,1,0:T(1,128)} async-done(((f32[64,1,4096]{2,1,0:T(1,128)}), f32[64,1,4096]{2,1,0:T(1,128)}, u32[]{:S(2)}, u32[]{:S(2)}) %all-to-all-start.3) | async-done | bytes 1048608 | tf_op jit(solution)/shard_map/all_to_all | solution.py:167
  428.3 6.5 %all-to-all-start.6 = ((f32[64,1,1536]{2,1,0:T(1,128)}), f32[64,1,1536]{2,1,0:T(1,128)S(1)}, u32[]{:S(2)}, u32[]{:S(2)}) async-start(f32[64,1,1536]{2,1,0:T(1,128)} %copy.29), calls=%async_computation.6 | async-start | bytes 786432 | tf_op jit(solution)/shard_map/all_to_all | solution.py:177
  434.7 2.3 fusion.12
  437.6 2.0 copy.27
  439.7 10.1 %all-to-all-done.6 = f32[64,1,1536]{2,1,0:T(1,128)S(1)} async-done(((f32[64,1,1536]{2,1,0:T(1,128)}), f32[64,1,1536]{2,1,0:T(1,128)S(1)}, u32[]{:S(2)}, u32[]{:S(2)}) %all-to-all-start.6) | async-done | bytes 393248 | tf_op jit(solution)/shard_map/all_to_all | solution.py:177
  449.8 5.8 all-to-all-start.4
  455.6 7.9 %convolution_convert_fusion = bf16[1024,2048]{1,0:T(8,128)(2,1)} fusion(bf16[1,768,2048]{2,1,0:T(8,128)(2,1)S(1)} %copy-done, f32[1024,768]{1,0:T(8,128)} %copy-done.2, f32[1024,768]{1,0:T(8,128)} %get-tuple-element.15), kind=kOutput, calls=%fused_computation.15 | convolution fusion | flops 3228041216 | bytes 13631488 | tf_op jit(solution)/shard_map/dot_general | solution.py:46
  463.5 20.0 %all-to-all-done.4 = f32[64,1,4096]{2,1,0:T(1,128)} async-done(((f32[64,1,4096]{2,1,0:T(1,128)}), f32[64,1,4096]{2,1,0:T(1,128)}, u32[]{:S(2)}, u32[]{:S(2)}) %all-to-all-start.4) | async-done | bytes 1048608 | tf_op jit(solution)/shard_map/all_to_all | solution.py:176
  483.5 6.7 %all-to-all-start.1 = ((bf16[64,16,2048]{2,1,0:T(8,128)(2,1)}), bf16[64,16,2048]{2,1,0:T(8,128)(2,1)}, u32[]{:S(2)}, u32[]{:S(2)}) async-start(bf16[64,16,2048]{2,1,0:T(8,128)(2,1)} %bitcast.86), calls=%async_computation.1 | async-start | bytes 8388608 | tf_op jit(solution)/shard_map/all_to_all | solution.py:132
  494.5 1.8 broadcast_in_dim_reshape.9
  496.3 88.2 %all-to-all-done.1 = bf16[64,16,2048]{2,1,0:T(8,128)(2,1)} async-done(((bf16[64,16,2048]{2,1,0:T(8,128)(2,1)}), bf16[64,16,2048]{2,1,0:T(8,128)(2,1)}, u32[]{:S(2)}, u32[]{:S(2)}) %all-to-all-start.1) | async-done | bytes 4194336 | tf_op jit(solution)/shard_map/all_to_all | solution.py:132
  584.6 11.7 %gather_fusion.1 = bf16[1024,2048]{1,0:T(8,128)(2,1)} fusion(bf16[1024,2048]{1,0:T(8,128)(2,1)} %bitcast.13, s32[1024]{0:T(1024)} %broadcast_clamp_fusion), kind=kCustom, calls=%fused_computation.1 | custom fusion | bytes 8392704 | tf_op jit(solution)/shard_map/gather | solution.py:140
  596.3 5.4 fusion.2
  601.7 2.3 copy.46
  (60 shorter events, 22.6 us)
Async XLA Ops:
  7.2 291.2 %copy-start = (bf16[1,768,2048]{2,1,0:T(8,128)(2,1)S(1)}, bf16[1,768,2048]{2,1,0:T(8,128)(2,1)}, u32[]{:S(2)}) copy-start(bf16[1,768,2048]{2,1,0:T(8,128)(2,1)} %param.17) | copy-start | bytes 9437188
  7.2 45.3 %copy-start.7 = (s32[64]{0:T(128)S(1)}, s32[64]{0:T(128)}, u32[]{:S(2)}) copy-start(s32[64]{0:T(128)} %param.15) | copy-start | bytes 772
  7.2 50.4 %copy-start.8 = (f32[128,8]{0,1:T(8,128)S(1)}, f32[128,8]{0,1:T(8,128)}, u32[]{:S(2)}) copy-start(f32[128,8]{0,1:T(8,128)} %param.13) | copy-start | bytes 12292
  57.7 14.7 %copy-start.4 = (f32[128,8]{1,0:T(8,128)}, f32[128,8]{1,0:T(8,128)S(1)}, u32[]{:S(2)}) copy-start(f32[128,8]{1,0:T(8,128)S(1)} %copy.24) | copy-start | bytes 12292
  196.6 101.8 %all-to-all-start.2 = ((bf16[64,16,2048]{2,1,0:T(8,128)(2,1)}), bf16[64,16,2048]{2,1,0:T(8,128)(2,1)}, u32[]{:S(2)}, u32[]{:S(2)}) async-start(bf16[64,16,2048]{2,1,0:T(8,128)(2,1)} %get-tuple-element.9), calls=%async_computation.2 | async-start | bytes 8388608 | tf_op jit(solution)/shard_map/all_to_all | solution.py:149
  203.8 164.9 %all-reduce.3.cloned.1.call-start = ((), (), s32[]{:S(2)}) async-start(), calls=%async_computation.7 | async-start | bytes 2883584 | tf_op jit(solution)/shard_map/psum | solution.py:165
  204.0 4.0 copy-start.1
  298.4 5.4 copy-start.3
  298.4 5.4 copy-start.6
  304.4 3.2 copy-start.2
  394.6 33.7 %all-to-all-start.3 = ((f32[64,1,4096]{2,1,0:T(1,128)}), f32[64,1,4096]{2,1,0:T(1,128)}, u32[]{:S(2)}, u32[]{:S(2)}) async-start(f32[64,1,4096]{2,1,0:T(1,128)} %get-tuple-element.5), calls=%async_computation.3 | async-start | bytes 2097152 | tf_op jit(solution)/shard_map/all_to_all | solution.py:167
  428.3 21.5 %all-to-all-start.6 = ((f32[64,1,1536]{2,1,0:T(1,128)}), f32[64,1,1536]{2,1,0:T(1,128)S(1)}, u32[]{:S(2)}, u32[]{:S(2)}) async-start(f32[64,1,1536]{2,1,0:T(1,128)} %copy.29), calls=%async_computation.6 | async-start | bytes 786432 | tf_op jit(solution)/shard_map/all_to_all | solution.py:177
  449.8 33.7 %all-to-all-start.4 = ((f32[64,1,4096]{2,1,0:T(1,128)}), f32[64,1,4096]{2,1,0:T(1,128)}, u32[]{:S(2)}, u32[]{:S(2)}) async-start(f32[64,1,4096]{2,1,0:T(1,128)} %copy.27), calls=%async_computation.4 | async-start | bytes 2097152 | tf_op jit(solution)/shard_map/all_to_all | solution.py:176
  483.5 101.1 %all-to-all-start.1 = ((bf16[64,16,2048]{2,1,0:T(8,128)(2,1)}), bf16[64,16,2048]{2,1,0:T(8,128)(2,1)}, u32[]{:S(2)}, u32[]{:S(2)}) async-start(bf16[64,16,2048]{2,1,0:T(8,128)(2,1)} %bitcast.86), calls=%async_computation.1 | async-start | bytes 8388608 | tf_op jit(solution)/shard_map/all_to_all | solution.py:132
  584.6 11.7 %copy-start.5 = (f32[128,8]{1,0:T(8,128)S(1)}, f32[128,8]{1,0:T(8,128)}, u32[]{:S(2)}) copy-start(f32[128,8]{1,0:T(8,128)} %copy-done.4) | copy-start | bytes 12292
Sparse Core Ops, SparseCore 0:
  316.8 51.7 all-reduce.2
where the time goes:
time: 615 us; the launch traced here: 611 us
  waiting for transfers between devices  276 us (45%)
  blocking collectives  133 us (22%)
  other arithmetic  56.1 us (9%)
  local copies, waits for them, and re-layouts  55.6 us (9%)
  matrix products  43 us (7%)
  starting transfers between devices  32.1 us (5%)
  between operations  14.3 us (2%)
    all_to_all x1, blocking collectives, body(): lax.all_to_all(rows_out, 'expert', split_axis=0, concat_axis=0, tiled=True)  107 us
    all_to_all x1, waiting for transfers between devices, body(): lax.all_to_all(layer_output.reshape(slot_total, capacity, model_feature_w...  88.2 us
    all_to_all x1, waiting for transfers between devices, body(): lax.all_to_all(scaled_out, 'expert', split_axis=0, concat_axis=0, tiled=T...  79.8 us
    psum x1, waiting for transfers between devices, body(): piece_a, piece_b = lax.psum((piece_a, piece_b), 'dp')  52 us
    another operation x3, other arithmetic  35.3 us
    all_to_all x1, waiting for transfers between devices, body(): lax.all_to_all(piece_a, 'expert', split_axis=0, concat_axis=0, tiled=True)  26.1 us
    all_to_all x1, blocking collectives, body(): lax.all_to_all(piece_b, 'expert', split_axis=0, concat_axis=0, tiled=True)  25.9 us
    all_to_all x1, waiting for transfers between devices, body(): lax.all_to_all(spread_a, 'expert', split_axis=0, concat_axis=0, tiled=True)  20 us
  transfers between devices with their start and end apart: 6, of which 6 were waited for; matrix products, arithmetic and copies ran while one was open for 6% of the time, Pallas kernels for 0%

commit v1 on v0

v1 whole, which is shorter than its diff:
```python
import jax
import jax.numpy as jnp
from jax import lax
from jax.sharding import PartitionSpec as P

ADAPTER_SCALE = 0.5
CAP = 16


def route_meta(routing, weights, choice, table):
    slots = table.shape[0]
    tok, top = routing.shape
    n = tok * top
    same = table[:, None] == table[None, :]
    ar = jnp.arange(slots, dtype=jnp.int32)
    occ = jnp.sum((same & (ar[None, :] < ar[:, None])).astype(jnp.int32), axis=1)
    cnt = jnp.sum(same.astype(jnp.int32), axis=1)
    holds = routing.reshape(n)[:, None] == table[None, :]
    wanted = choice.reshape(n)[:, None] % cnt[None, :]
    picked = holds & (wanted == occ[None, :])
    rows = lax.broadcasted_iota(jnp.int32, (n, n), 0)
    cols = lax.broadcasted_iota(jnp.int32, (n, n), 1)
    tri = (cols < rows).astype(jnp.bfloat16)
    ahead = jnp.dot(tri, picked.astype(jnp.bfloat16), preferred_element_type=jnp.float32)
    rank = jnp.where(picked, ahead, -1.0)
    hit = rank[:, None, :] == jnp.arange(CAP, dtype=jnp.float32)[None, :, None]
    token = (jnp.arange(n, dtype=jnp.int32) // top + 1).astype(jnp.float32)
    src = jnp.sum(jnp.where(hit, token[:, None, None], 0.0), axis=0) - 1.0
    wgt = jnp.sum(jnp.where(hit, weights.reshape(n)[:, None, None], 0.0), axis=0)
    return src.T, wgt.T


def body(tokens, cotangent, routing, weights, choice, table, gate_up, down, amap, bmap):
    slots = lax.axis_size("expert")
    n_dp = lax.axis_size("dp")
    tok, width = tokens.shape
    gate_up, down, amap, bmap = gate_up[0], down[0], amap[0], bmap[0]
    rank, ff = bmap.shape[1:]
    src, wgt = route_meta(routing, weights, choice, table)
    src, wgt = src.reshape(-1), wgt.reshape(-1)
    total = src.shape[0]
    tid = jnp.arange(tok, dtype=jnp.float32)
    onehot = (src[:, None] == tid[None, :]).astype(jnp.bfloat16)
    rows_out = jnp.dot(onehot, tokens, preferred_element_type=jnp.float32).astype(jnp.bfloat16)
    scaled_out = (
        jnp.dot(onehot, cotangent, preferred_element_type=jnp.float32) * wgt[:, None]
    ).astype(jnp.bfloat16)

    def exchange(v):
        return lax.all_to_all(v, "expert", split_axis=0, concat_axis=0, tiled=True)

    x = exchange(rows_out)
    low = jnp.dot(x, amap, preferred_element_type=jnp.float32).astype(jnp.bfloat16)
    pre = jnp.dot(x, gate_up, preferred_element_type=jnp.float32)
    pre_gate = pre[:, :ff] + ADAPTER_SCALE * jnp.dot(
        low[:, :rank], bmap[0], preferred_element_type=jnp.float32
    )
    pre_up = pre[:, ff:] + ADAPTER_SCALE * jnp.dot(
        low[:, rank:], bmap[1], preferred_element_type=jnp.float32
    )
    sig = jax.nn.sigmoid(pre_gate)
    act = pre_gate * sig
    hidden = (act * pre_up).astype(jnp.bfloat16)
    out = jnp.dot(hidden, down, preferred_element_type=jnp.float32).astype(jnp.bfloat16)
    ret = exchange(out)
    wmat = jnp.where(src[None, :] == tid[:, None], wgt[None, :], 0.0)
    w_hi = wmat.astype(jnp.bfloat16)
    w_lo = (wmat - w_hi.astype(jnp.float32)).astype(jnp.bfloat16)
    mixed = (
        jnp.dot(w_hi, ret, preferred_element_type=jnp.float32)
        + jnp.dot(w_lo, ret, preferred_element_type=jnp.float32)
    ).astype(jnp.bfloat16)

    scaled = exchange(scaled_out)
    back = lax.dot_general(scaled, down, (((1,), (1,)), ((), ())), preferred_element_type=jnp.float32)
    g_up = (back * act).astype(jnp.bfloat16)
    g_gate = (back * pre_up * (sig * (1.0 + pre_gate * (1.0 - sig)))).astype(jnp.bfloat16)
    rdims = (((0,), (0,)), ((), ()))
    cdims = (((1,), (1,)), ((), ()))
    gb0 = ADAPTER_SCALE * lax.dot_general(low[:, :rank], g_gate, rdims, preferred_element_type=jnp.float32)
    gb1 = ADAPTER_SCALE * lax.dot_general(low[:, rank:], g_up, rdims, preferred_element_type=jnp.float32)
    lg0 = lax.dot_general(g_gate, bmap[0], cdims, preferred_element_type=jnp.float32)
    lg1 = lax.dot_general(g_up, bmap[1], cdims, preferred_element_type=jnp.float32)
    low_grad = (ADAPTER_SCALE * jnp.concatenate([lg0, lg1], axis=1)).astype(jnp.bfloat16)
    ga = lax.dot_general(x, low_grad, rdims, preferred_element_type=jnp.float32)
    gb = jnp.concatenate([gb0, gb1], axis=0)
    lanes = 2 * rank
    grads = jnp.concatenate(
        [ga] + [gb[:, i * lanes : (i + 1) * lanes] for i in range(ff // lanes)], axis=0
    )
    part = lax.psum_scatter(grads, "dp", scatter_dimension=0, tiled=True)
    piece = part.reshape(slots, -1)
    got = exchange(piece)
    same = (table[:, None] == table[None, :]).astype(jnp.float32)
    summed = jnp.dot(same, got, precision=lax.Precision.HIGHEST)
    mine = exchange(summed).reshape(part.shape)
    full = lax.all_gather(mine, "dp", axis=0, tiled=True)
    grad_a = full[:width]
    grad_b = jnp.concatenate(
        [full[width + i * lanes : width + (i + 1) * lanes] for i in range(ff // lanes)], axis=1
    )
    return mixed, grad_a[None], grad_b.reshape(1, 2, rank, ff)


def solution(mesh):
    both = P(("dp", "expert"), None)
    return jax.shard_map(
        body,
        mesh=mesh,
        in_specs=(both, both, both, both, both, P(), P("expert", None, None), P("expert", None, None),
                  P("expert", None, None), P("expert", None, None, None)),
        out_specs=(both, P("expert", None, None), P("expert", None, None, None)),
        check_vma=False,
    )
```

time: 615 us -> 440 us (0.72)
  blocking collectives: 133 us -> 26.7 us
  other arithmetic: 56.1 us -> 5.71 us
  local copies, waits for them, and re-layouts: 55.6 us -> 15.9 us
  matrix products: 43 us -> 60.7 us
  waiting for transfers between devices: 276 us -> 283 us
    all_to_all x2 -> x1, blocking collectives: 133 us -> 26.7 us  [exchange(): return lax.all_to_all(v, 'expert', split_axis=0, concat_axis=0, tiled=True)]
    psum x1 -> x0, waiting for transfers between devices: 52 us -> none  [body(): piece_a, piece_b = lax.psum((piece_a, piece_b), 'dp')]
    another operation x5 -> x0, other arithmetic: 36.5 us -> none
    gather x4 -> x0, local copies, waits for them, and re-layouts: 36.1 us -> none  [the longest x1 11.7 us: body(): picked_rows = returned[jnp.minimum(dest_index, slot_total * capacity - 1)]]
    all_gather x0 -> x1, waiting for transfers between devices: none -> 29.7 us  [body(): full = lax.all_gather(mine, 'dp', axis=0, tiled=True)]
    reduce_scatter x0 -> x1, waiting for transfers between devices: none -> 24.1 us  [body(): part = lax.psum_scatter(grads, 'dp', scatter_dimension=0, tiled=True)]
    dot_general x15 -> x17, matrix products: 43 us -> 60.7 us  [the longest x1 11.7 us: body(): pre = jnp.dot(x, gate_up, preferred_element_type=jnp.float32)]
    select_n x4 -> x1, other arithmetic: 7.44 us -> 0.01 us  [route_meta(): wanted = choice.reshape(n)[:, None] % cnt[None, :]]
  transfers between devices with their start and end apart: 6 -> 6, of which waited for: 6 -> 6; matrix products, arithmetic and copies ran while one was open for 6% -> 9% of each run, Pallas kernels for 0% -> 0%
where the time goes in v1:
time: 440 us; the launch traced here: 438 us
  waiting for transfers between devices  283 us (64%)
  matrix products  60.7 us (14%)
  starting transfers between devices  31.9 us (7%)
  blocking collectives  26.7 us (6%)
  local copies, waits for them, and re-layouts  15.9 us (4%)
  between operations  14.2 us (3%)
  other arithmetic  5.71 us (1%)
    all_to_all x4, waiting for transfers between devices, exchange(): return lax.all_to_all(v, 'expert', split_axis=0, concat_axis=0, tiled=True)  228 us
    all_to_all x4, starting transfers between devices, exchange(): return lax.all_to_all(v, 'expert', split_axis=0, concat_axis=0, tiled=True)  31.6 us
    all_gather x1, waiting for transfers between devices, body(): full = lax.all_gather(mine, 'dp', axis=0, tiled=True)  29.7 us
    all_to_all x1, blocking collectives, exchange(): return lax.all_to_all(v, 'expert', split_axis=0, concat_axis=0, tiled=True)  26.7 us
    reduce_scatter x1, waiting for transfers between devices, body(): part = lax.psum_scatter(grads, 'dp', scatter_dimension=0, tiled=True)  24.1 us
    dot_general x1, matrix products, body(): pre = jnp.dot(x, gate_up, preferred_element_type=jnp.float32)  11.7 us
    unnamed x20, local copies, waits for them, and re-layouts  10.5 us
  transfers between devices with their start and end apart: 6, of which 6 were waited for; matrix products, arithmetic and copies ran while one was open for 9% of the time, Pallas kernels for 0%

profile of v1, /device:TPU:1, one launch (start us, length us, event | category | flops | bytes accessed | tf_op | source)
XLA Modules:
  0.0 437.8 jit_solution(17938053177269556972)
XLA Ops:
  7.2 1.0 fusion.67
  10.9 6.0 %fusion.8 = f32[1024,64]{0,1:T(8,128)S(1)} fusion(s32[64]{0:T(128)S(1)} %get-tuple-element.6, s32[64]{0:T(128)S(1)} %compare_select_fusion, s32[1024]{0:T(1024)S(1)} %rem.30, s32[1024]{0:T(1024)S(1)} %eq.96, s32[64]{0:T(128)} %param.15, pred[64]{0:T(512)(128)(4,1)S(1)} %broadcast_compare_fusion), kind=kOutput, calls=%fused_computation.25 | convolution fusion | flops 136642560 | bytes 271168 | tf_op jit(solution)/shard_map/dot_general | solution.py:24
  16.8 0.9 select_reduce_fusion
  17.9 4.3 convolution_convert_fusion.1
  22.2 13.2 %all-to-all-start = ((bf16[64,16,2048]{2,1,0:T(8,128)(2,1)}), bf16[64,16,2048]{2,1,0:T(8,128)(2,1)}, u32[]{:S(2)}, u32[]{:S(2)}) async-start(bf16[64,16,2048]{2,1,0:T(8,128)(2,1)} %bitcast.55), calls=%async_computation | async-start | bytes 8388608 | tf_op jit(solution)/shard_map/all_to_all | solution.py:50
  35.6 4.4 %multiply_convert_fusion = bf16[1024,2048]{1,0:T(8,128)(2,1)} fusion(bf16[128,2048]{1,0:T(8,128)(2,1)} %param.11, f32[1024]{0:T(1024)S(1)} %broadcast_in_dim.65, f32[1024]{0:T(1024)S(1)} %eq.109), kind=kOutput, calls=%fused_computation | convolution fusion | flops 541196288 | bytes 4726784 | tf_op jit(solution)/shard_map/dot_general | solution.py:46
  40.0 89.8 %all-to-all-done = bf16[64,16,2048]{2,1,0:T(8,128)(2,1)} async-done(((bf16[64,16,2048]{2,1,0:T(8,128)(2,1)}), bf16[64,16,2048]{2,1,0:T(8,128)(2,1)}, u32[]{:S(2)}, u32[]{:S(2)}) %all-to-all-start) | async-done | bytes 4194336 | tf_op jit(solution)/shard_map/all_to_all | solution.py:50
  129.8 7.4 %all-to-all-start.2 = ((bf16[64,16,2048]{2,1,0:T(8,128)(2,1)}), bf16[64,16,2048]{2,1,0:T(8,128)(2,1)}, u32[]{:S(2)}, u32[]{:S(2)}) async-start(bf16[64,16,2048]{2,1,0:T(8,128)(2,1)} %bitcast.54), calls=%async_computation.2 | async-start | bytes 8388608 | tf_op jit(solution)/shard_map/all_to_all | solution.py:50
  137.4 3.8 convolution_convert_fusion.2
  141.2 11.7 %fusion = f32[1024,1536]{1,0:T(8,128)} fusion(bf16[1024,2048]{1,0:T(8,128)(2,1)} %bitcast.3, bf16[1,2048,1536]{2,1,0:T(8,128)(2,1)} %param.16), kind=kOutput, calls=%fused_computation.1 | convolution fusion | flops 6442450944 | bytes 16777216 | tf_op jit(solution)/shard_map/dot_general | solution.py:54
  152.9 78.9 %all-to-all-done.2 = bf16[64,16,2048]{2,1,0:T(8,128)(2,1)} async-done(((bf16[64,16,2048]{2,1,0:T(8,128)(2,1)}), bf16[64,16,2048]{2,1,0:T(8,128)(2,1)}, u32[]{:S(2)}, u32[]{:S(2)}) %all-to-all-start.2) | async-done | bytes 4194336 | tf_op jit(solution)/shard_map/all_to_all | solution.py:50
  231.9 5.4 %fusion.3 = f32[1024,768]{1,0:T(8,128)S(1)} fusion(bf16[1024,2048]{1,0:T(8,128)(2,1)} %bitcast.12, bf16[1,768,2048]{2,1,0:T(8,128)(2,1)S(1)} %copy-done), kind=kOutput, calls=%fused_computation.12 | convolution fusion | flops 3221225472 | bytes 10485760 | tf_op jit(solution)/shard_map/dot_general | solution.py:75
  237.9 3.1 multiply_convert_fusion.2
  243.0 4.5 %convolution_dynamic-update-slice_fusion = f32[2816,128]{1,0:T(8,128)} fusion(bf16[1024,2048]{1,0:T(8,128)(2,1)} %bitcast.3, f32[1024,64]{0,1:T(8,128)S(1)} %fusion.45, f32[1024,64]{0,1:T(8,128)S(1)} %fusion.48), kind=kOutput, calls=%fused_computation.20 | convolution fusion | flops 537264128 | bytes 5767168 | tf_op jit(solution)/shard_map/dot_general | solution.py:85
  251.3 24.1 %reduce-scatter.2.cloned.1.call-done = f32[704,128]{1,0:T(8,128)} async-done(((f32[2816,128]{1,0:T(8,128)}), f32[704,128]{1,0:T(8,128)}) %reduce-scatter.2.cloned.1.call-update) | async-done | bytes 360464 | tf_op jit(solution)/shard_map/reduce_scatter | solution.py:91
  275.4 26.7 %all_to_all.57 = f32[64,1,1408]{2,1,0:T(1,128)S(1)} all-to-all(f32[64,1,1408]{2,1,0:T(1,128)} %bitcast.58), channel_id=1, replica_groups=mesh['dp'=4,'expert'=64] {'expert'}, dimensions={0} | all-to-all | bytes 720896 | tf_op jit(solution)/shard_map/all_to_all | solution.py:50
  302.5 1.1 copy.30
  303.6 5.4 %all-to-all-start.4 = ((f32[64,1,1408]{2,1,0:T(1,128)}), f32[64,1,1408]{2,1,0:T(1,128)S(1)}, u32[]{:S(2)}, u32[]{:S(2)}) async-start(f32[64,1,1408]{2,1,0:T(1,128)} %copy.30), calls=%async_computation.5 | async-start | bytes 720896 | tf_op jit(solution)/shard_map/all_to_all | solution.py:50
  309.0 7.9 %convolution_convert_fusion = bf16[1024,2048]{1,0:T(8,128)(2,1)} fusion(bf16[1,768,2048]{2,1,0:T(8,128)(2,1)S(1)} %copy-done, f32[1024,768]{1,0:T(8,128)} %copy-done.1, f32[1024,768]{1,0:T(8,128)} %get-tuple-element.9), kind=kOutput, calls=%fused_computation.8 | convolution fusion | flops 3228041216 | bytes 13631488 | tf_op jit(solution)/shard_map/dot_general | solution.py:64
  316.9 6.6 %all-to-all-done.4 = f32[64,1,1408]{2,1,0:T(1,128)S(1)} async-done(((f32[64,1,1408]{2,1,0:T(1,128)}), f32[64,1,1408]{2,1,0:T(1,128)S(1)}, u32[]{:S(2)}, u32[]{:S(2)}) %all-to-all-start.4) | async-done | bytes 360480 | tf_op jit(solution)/shard_map/all_to_all | solution.py:50
  324.3 5.6 %all-to-all-start.1 = ((bf16[64,16,2048]{2,1,0:T(8,128)(2,1)}), bf16[64,16,2048]{2,1,0:T(8,128)(2,1)}, u32[]{:S(2)}, u32[]{:S(2)}) async-start(bf16[64,16,2048]{2,1,0:T(8,128)(2,1)} %bitcast.56), calls=%async_computation.1 | async-start | bytes 8388608 | tf_op jit(solution)/shard_map/all_to_all | solution.py:50
  330.7 29.7 %all-gather.2.cloned.1.call-done = f32[2816,128]{1,0:T(8,128)} async-done(((f32[704,128]{1,0:T(8,128)}), f32[2816,128]{1,0:T(8,128)}) %all-gather.2.cloned.1.call-update) | async-done | bytes 1441808 | tf_op jit(solution)/shard_map/all_gather | solution.py:97
  360.4 1.5 slice_dynamic-update-slice_fusion.5
  361.8 1.5 slice_dynamic-update-slice_fusion.4
  363.3 1.5 slice_dynamic-update-slice_fusion.3
  364.8 1.5 slice_dynamic-update-slice_fusion.2
  366.2 1.5 slice_dynamic-update-slice_fusion.1
  367.7 1.5 slice_dynamic-update-slice_fusion
  369.2 2.3 slice_bitcast_fusion
  371.5 52.9 %all-to-all-done.1 = bf16[64,16,2048]{2,1,0:T(8,128)(2,1)} async-done(((bf16[64,16,2048]{2,1,0:T(8,128)(2,1)}), bf16[64,16,2048]{2,1,0:T(8,128)(2,1)}, u32[]{:S(2)}, u32[]{:S(2)}) %all-to-all-start.1) | async-done | bytes 4194336 | tf_op jit(solution)/shard_map/all_to_all | solution.py:50
  424.3 2.9 fusion.15
  427.2 3.8 fusion.7
  (42 shorter events, 11.4 us)
Async XLA Ops:
  7.2 224.7 %copy-start = (bf16[1,768,2048]{2,1,0:T(8,128)(2,1)S(1)}, bf16[1,768,2048]{2,1,0:T(8,128)(2,1)}, u32[]{:S(2)}) copy-start(bf16[1,768,2048]{2,1,0:T(8,128)(2,1)} %param.17) | copy-start | bytes 9437188
  22.2 107.6 %all-to-all-start = ((bf16[64,16,2048]{2,1,0:T(8,128)(2,1)}), bf16[64,16,2048]{2,1,0:T(8,128)(2,1)}, u32[]{:S(2)}, u32[]{:S(2)}) async-start(bf16[64,16,2048]{2,1,0:T(8,128)(2,1)} %bitcast.55), calls=%async_computation | async-start | bytes 8388608 | tf_op jit(solution)/shard_map/all_to_all | solution.py:50
  129.8 102.0 %all-to-all-start.2 = ((bf16[64,16,2048]{2,1,0:T(8,128)(2,1)}), bf16[64,16,2048]{2,1,0:T(8,128)(2,1)}, u32[]{:S(2)}, u32[]{:S(2)}) async-start(bf16[64,16,2048]{2,1,0:T(8,128)(2,1)} %bitcast.54), calls=%async_computation.2 | async-start | bytes 8388608 | tf_op jit(solution)/shard_map/all_to_all | solution.py:50
  137.2 138.2 %reduce-scatter.2.cloned.1.call-start = ((), (), s32[]{:S(2)}) async-start(), calls=%async_computation.6 | async-start | bytes 1802240 | tf_op jit(solution)/shard_map/reduce_scatter | solution.py:91
  231.8 5.4 %copy-start.2 = (f32[1024,1536]{1,0:T(8,128)S(1)}, f32[1024,1536]{1,0:T(8,128)}, u32[]{:S(2)}) copy-start(f32[1024,1536]{1,0:T(8,128)} %fusion) | copy-start | bytes 18874372
  231.9 5.5 %copy-start.4 = (bf16[1,2,64,768]{3,2,1,0:T(8,128)(2,1)S(1)}, bf16[1,2,64,768]{3,2,1,0:T(8,128)(2,1)}, u32[]{:S(2)}) copy-start(bf16[1,2,64,768]{3,2,1,0:T(8,128)(2,1)} %param.19) | copy-start | bytes 589828
  237.9 3.1 copy-start.1
  247.5 54.6 %copy-start.5 = (s32[64]{0:T(128)S(1)}, s32[64]{0:T(128)}, u32[]{:S(2)}) copy-start(s32[64]{0:T(128)} %param.15) | copy-start | bytes 772
  303.6 20.0 %all-to-all-start.4 = ((f32[64,1,1408]{2,1,0:T(1,128)}), f32[64,1,1408]{2,1,0:T(1,128)S(1)}, u32[]{:S(2)}, u32[]{:S(2)}) async-start(f32[64,1,1408]{2,1,0:T(1,128)} %copy.30), calls=%async_computation.5 | async-start | bytes 720896 | tf_op jit(solution)/shard_map/all_to_all | solution.py:50
  323.5 0.7 copy-start.3
  324.3 100.0 %all-to-all-start.1 = ((bf16[64,16,2048]{2,1,0:T(8,128)(2,1)}), bf16[64,16,2048]{2,1,0:T(8,128)(2,1)}, u32[]{:S(2)}, u32[]{:S(2)}) async-start(bf16[64,16,2048]{2,1,0:T(8,128)(2,1)} %bitcast.56), calls=%async_computation.1 | async-start | bytes 8388608 | tf_op jit(solution)/shard_map/all_to_all | solution.py:50
  329.9 30.4 %all-gather.2.cloned.1.call-start = ((), (), s32[]{:S(2)}) async-start(), calls=%async_computation.7 | async-start | bytes 1802240 | tf_op jit(solution)/shard_map/all_gather | solution.py:97
Sparse Core Ops, SparseCore 0:
  251.4 23.9 reduce-scatter.1
  333.1 27.1 all-gather.1

commit v2 on v1

v2 whole, which is shorter than its diff:
```python
import jax
import jax.numpy as jnp
from jax import lax
from jax.experimental import pallas as pl
from jax.experimental.pallas import tpu as pltpu
from jax.sharding import PartitionSpec as P

ADAPTER_SCALE = 0.5
CAP = 16
ROW = 8
NZ = 8
BLK = 128
F32 = jnp.float32
BF16 = jnp.bfloat16
MESH = pl.DeviceIdType.MESH
RIGHT, LEFT = 0, 1


def route_meta(routing, weights, choice, table):
    slots = table.shape[0]
    tok, top = routing.shape
    n = tok * top
    same = table[:, None] == table[None, :]
    ar = jnp.arange(slots, dtype=jnp.int32)
    occ = jnp.sum((same & (ar[None, :] < ar[:, None])).astype(jnp.int32), axis=1)
    cnt = jnp.sum(same.astype(jnp.int32), axis=1)
    holds = routing.reshape(n)[:, None] == table[None, :]
    wanted = choice.reshape(n)[:, None] % cnt[None, :]
    picked = holds & (wanted == occ[None, :])
    rows = lax.broadcasted_iota(jnp.int32, (n, n), 0)
    cols = lax.broadcasted_iota(jnp.int32, (n, n), 1)
    tri = (cols < rows).astype(BF16)
    ahead = jnp.dot(tri, picked.astype(BF16), preferred_element_type=F32)
    rank = jnp.where(picked, ahead, -1.0)
    hit = rank[:, None, :] == jnp.arange(CAP, dtype=F32)[None, :, None]
    token = (jnp.arange(n, dtype=jnp.int32) // top + 1).astype(F32)
    src = jnp.sum(jnp.where(hit, token[:, None, None], 0.0), axis=0) - 1.0
    wgt = jnp.sum(jnp.where(hit, weights.reshape(n)[:, None, None], 0.0), axis=0)
    return src.T, wgt.T


def dot(a, b):
    return jnp.dot(a, b, preferred_element_type=F32)


def dot_t(a, b):
    return lax.dot_general(a, b, (((1,), (1,)), ((), ())), preferred_element_type=F32)


def t_dot(a, b):
    return lax.dot_general(a, b, (((0,), (0,)), ((), ())), preferred_element_type=F32)


def ds(i, n):
    return pl.ds(pl.multiple_of(i * n, n), n)


def kernel(
    tokens, cots, meta, pmat, gate_up, down, amap, bmap,
    mixed_out, grads_out,
    ring, metar, pick, wcol, xs, xr, outs, rets, rsr, mix,
    gu, dn, am, bm, low, act, mul, hid, grad,
    ysend, yrecv, t1, r1, r2, r2f, rb2, rb1, yq, yo,
    ld, ag_s, ag_r, mt_s, mt_r, x_s, x_r, rt_s, rt_r, rs_s, rs_r, y_s, y_r, g_s, g_r, st,
):
    width = tokens.shape[1]
    ff = dn.shape[0]
    rank2 = am.shape[1]
    n_dp = yrecv.shape[0] + 1
    part = rank2 // n_dp
    dp = lax.axis_index("dp")
    e = lax.axis_index("expert")
    z, j = e // ROW, e % ROW

    def zdev(step):
        return (dp, lax.rem(z + step + NZ, NZ) * ROW + j)

    def rowdev(i):
        return (dp, z * ROW + i)

    def dpdev(i):
        return (i, e)

    bar = pltpu.get_barrier_semaphore()
    for s in range(1, NZ):
        pl.semaphore_signal(bar, inc=1, device_id=zdev(s), device_id_type=MESH)
    for s in range(1, ROW):
        pl.semaphore_signal(bar, inc=1, device_id=rowdev(lax.rem(j + s, ROW)), device_id_type=MESH)
    for s in range(1, n_dp):
        pl.semaphore_signal(bar, inc=1, device_id=dpdev(lax.rem(dp + s, n_dp)), device_id_type=MESH)

    half = rank2 // 2
    loads = [
        pltpu.make_async_copy(tokens, ring.at[0, 0], ld.at[0]),
        pltpu.make_async_copy(cots, ring.at[1, 0], ld.at[1]),
        pltpu.make_async_copy(gate_up, gu, ld.at[2]),
        pltpu.make_async_copy(down, dn, ld.at[3]),
        pltpu.make_async_copy(amap, am, ld.at[4]),
        pltpu.make_async_copy(bmap.at[0], bm.at[0, pl.ds(0, half)], ld.at[5]),
        pltpu.make_async_copy(bmap.at[1], bm.at[1, pl.ds(half, half)], ld.at[6]),
    ]
    for c in loads:
        c.start()
    bm[0, half:, :] = jnp.zeros((half, ff), BF16)
    bm[1, :half, :] = jnp.zeros((half, ff), BF16)
    metar[0] = meta[z]
    pl.semaphore_wait(bar, NZ - 1 + ROW - 1 + n_dp - 1)

    def copy_to(src, dst, send, recv, device):
        return pltpu.make_async_remote_copy(
            src_ref=src, dst_ref=dst, send_sem=send, recv_sem=recv, device_id=device, device_id_type=MESH
        )

    def wait_bytes(ref, sem):
        pltpu.make_async_copy(ref, ref, sem).wait()

    def ring_copy(a, way, k):
        if way == RIGHT:
            frm, to, dev = (0 if k == 1 else 2 * k - 3), 2 * k - 1, zdev(1)
        else:
            frm, to, dev = 2 * k - 2, min(2 * k, NZ - 1), zdev(-1)
        src, dst = ring.at[a, frm], ring.at[a, to]
        if k == NZ // 2:
            rows = pl.ds(0 if way == RIGHT else BLK // 2, BLK // 2)
            src, dst = src.at[rows], dst.at[rows]
        return copy_to(src, dst, ag_s.at[a, way, k - 1], ag_r.at[a, way, k - 1], dev)

    def ring_start(a, k):
        ring_copy(a, RIGHT, k).start()
        ring_copy(a, LEFT, k).start()

    loads[0].wait()
    ring_start(0, 1)

    def meta_copy(s):
        place = 2 * s - 1 if s <= NZ // 2 else 2 * (NZ - s)
        dst_row = lax.rem(z + s, NZ)
        return place, copy_to(meta.at[dst_row], metar.at[place], mt_s.at[place], mt_r.at[place], zdev(s))

    metas = dict(meta_copy(s) for s in range(1, NZ))
    for c in metas.values():
        c.start()

    def prepare(p):
        srow = jnp.broadcast_to(metar[p, 0:1, :], (BLK, BLK))
        wrow = jnp.broadcast_to(metar[p, 1:2, :], (BLK, BLK))
        lane = lax.broadcasted_iota(jnp.int32, (BLK, BLK), 1).astype(F32)
        pick[p] = (srow.T == lane).astype(BF16)
        wcol[p] = wrow.T

    CT = 512

    def relay(a, p):
        def tile(i, carry):
            v = dot(pick[p], ring[a, p, :, ds(i, CT)])
            if a == 1:
                v = v * wcol[p][:, 0:1]
            xs[a, p, :, ds(i, CT)] = v.astype(BF16)
            return carry

        lax.fori_loop(0, width // CT, tile, 0)
        row_send(xs.at[a, p], xr.at[a, p], x_s.at[a, p], x_r.at[a, p])

    def row_send(src, dst, send, recv):
        mine = ds(j, CAP)
        for s in range(1, ROW):
            to = lax.rem(j + s, ROW)
            copy_to(src.at[ds(to, CAP)], dst.at[mine], send, recv, rowdev(to)).start()
        pltpu.make_async_copy(src.at[mine], dst.at[mine], recv).start()

    def row_sent(src, send):
        wait_bytes(src.at[pl.ds(0, (ROW - 1) * CAP)], send)

    FT = 256
    CH = 256

    def forward(c):
        for p in (2 * c, 2 * c + 1):
            wait_bytes(xr.at[0, p], x_r.at[0, p])
        rows = pl.ds(c * CH, CH)
        x = xr.at[0, pl.ds(2 * c, 2)]

        def xv():
            return x[...].reshape(CH, width)

        low[rows, :] = dot(xv(), am[...]).astype(BF16)

        def tile(f, carry):
            cols = ds(f, FT)
            up_cols = pl.ds(pl.multiple_of(ff + f * FT, FT), FT)
            lw = low[rows, :]
            pg = dot(xv(), gu[:, cols]) + ADAPTER_SCALE * dot(lw, bm[0, :, cols])
            pu = dot(xv(), gu[:, up_cols]) + ADAPTER_SCALE * dot(lw, bm[1, :, cols])
            sig = jax.nn.sigmoid(pg)
            ac = pg * sig
            act[rows, cols] = ac
            mul[rows, cols] = pu * (sig * (1.0 + pg * (1.0 - sig)))
            hid[:, cols] = (ac * pu).astype(BF16)
            return carry

        lax.fori_loop(0, ff // FT, tile, 0)

        def otile(i, carry):
            cols = ds(i, CT)
            o = dot(hid[...], dn[:, cols]).astype(BF16)
            outs[2 * c, :, cols] = o[:BLK]
            outs[2 * c + 1, :, cols] = o[BLK:]
            return carry

        lax.fori_loop(0, width // CT, otile, 0)

    def backward(c):
        for p in (2 * c, 2 * c + 1):
            wait_bytes(xr.at[1, p], x_r.at[1, p])
        rows = pl.ds(c * CH, CH)

        def tile(f, lg):
            cols = ds(f, FT)
            gcols = pl.ds(pl.multiple_of(width + f * FT, FT), FT)
            back = dot_t(xr[1, pl.ds(2 * c, 2)].reshape(CH, width), dn[cols, :])
            g_up = (back * act[rows, cols]).astype(BF16)
            g_gate = (back * mul[rows, cols]).astype(BF16)
            lw = low[rows, :]
            gb0 = ADAPTER_SCALE * t_dot(lw, g_gate)
            gb1 = ADAPTER_SCALE * t_dot(lw, g_up)
            gb = jnp.concatenate([gb0[:half], gb1[half:]], axis=0)
            if c == 0:
                grad[:, gcols] = gb
            else:
                grad[:, gcols] += gb
            return lg + dot_t(g_gate, bm[0, :, cols]) + dot_t(g_up, bm[1, :, cols])

        lg = lax.fori_loop(0, ff // FT, tile, jnp.zeros((CH, rank2), F32))
        lgb = (ADAPTER_SCALE * lg).astype(BF16)

        def gtile(i, carry):
            cols = ds(i, CT)
            ga = t_dot(lgb, xr[0, pl.ds(2 * c, 2), :, cols].reshape(CH, CT))
            if c == 0:
                grad[:, cols] = ga
            else:
                grad[:, cols] += ga
            return carry

        lax.fori_loop(0, width // CT, gtile, 0)

    def places(k):
        return (0,) if k == 0 else (7,) if k == NZ // 2 else (2 * k - 1, 2 * k)

    loads[1].wait()
    for a in (0, 1):
        for k in range(NZ // 2 + 1):
            if k > 0:
                ring_copy(a, RIGHT, k).wait_recv()
                ring_copy(a, LEFT, k).wait_recv()
                if k < NZ // 2:
                    ring_start(a, k + 1)
            if a == 0 and k == NZ // 2 - 1:
                ring_start(1, 1)
            for p in places(k):
                if a == 0:
                    if p > 0:
                        metas[p].wait_recv()
                    prepare(p)
                relay(a, p)
            if a == 0 and k == 1:
                for c in loads[2:]:
                    c.wait()
            if k >= 2:
                (forward if a == 0 else backward)(k - 2)
            if a == 1 and k == 0:
                forward(3)

    def ret_start(k):
        for p in places(k):
            row_send(outs.at[p], rets.at[p], rt_s.at[p], rt_r.at[p])

    ret_start(4)
    ret_start(3)
    backward(3)

    def gcast(i, carry):
        cols = ds(i, 256)
        ysend[:, cols] = grad[:, cols].astype(BF16)
        return carry

    lax.fori_loop(0, grad.shape[1] // 256, gcast, 0)

    for s in range(1, n_dp):
        to = lax.rem(dp + s, n_dp)
        copy_to(ysend.at[ds(to, part)], yrecv.at[s - 1], y_s.at[0], y_r.at[0], dpdev(to)).start()

    for p in range(NZ):
        row_sent(xs.at[0, p], x_s.at[0, p])

    def partial(p, store):
        wait_bytes(rets.at[p], rt_r.at[p])
        srow = metar[p, 0:1, :]
        tid = lax.broadcasted_iota(jnp.int32, (BLK, BLK), 0).astype(F32)
        w = jnp.where(tid == srow, metar[p, 1:2, :], 0.0)
        hi = w.astype(BF16)
        lo = (w - hi.astype(F32)).astype(BF16)

        def tile(i, carry):
            cols = ds(i, CT)
            r = rets[p, :, cols]
            store(cols, dot(hi, r) + dot(lo, r))
            return carry

        lax.fori_loop(0, width // CT, tile, 0)

    def rs_copy(way, k):
        if k == 1:
            rows = pl.ds(0 if way == RIGHT else BLK // 2, BLK // 2)
            src, dst = xs.at[0, 7, rows], rsr.at[way, 0, rows]
        else:
            p = 2 * (NZ // 2 + 1 - k) - (0 if way == RIGHT else 1)
            src, dst = xs.at[0, p], rsr.at[way, k - 1]
        return copy_to(src, dst, rs_s.at[way, k - 1], rs_r.at[way, k - 1], zdev(1 if way == RIGHT else -1))

    def rs_step(k):
        if k == 1:
            def store(cols, v):
                xs[0, 7, :, cols] = v.astype(BF16)

            partial(7, store)
            for way in (RIGHT, LEFT):
                rs_copy(way, 1).start()
            return
        for way in (RIGHT, LEFT):
            p = 2 * (NZ // 2 + 1 - k) - (0 if way == RIGHT else 1)
            rs_copy(way, k - 1).wait_recv()

            def store(cols, v, p=p, way=way):
                if k == 2:
                    h = BLK // 2
                    mine = slice(0, h) if way == RIGHT else slice(h, BLK)
                    rest = slice(h, BLK) if way == RIGHT else slice(0, h)
                    xs[0, p, mine, cols] = (v[mine] + rsr[way, 0, mine, cols].astype(F32)).astype(BF16)
                    xs[0, p, rest, cols] = v[rest].astype(BF16)
                else:
                    xs[0, p, :, cols] = (v + rsr[way, k - 2, :, cols].astype(F32)).astype(BF16)

            partial(p, store)
            rs_copy(way, k).start()

    rs_step(1)
    ret_start(2)

    wait_bytes(yrecv, y_r.at[0])
    ncol = grad.shape[1] // 128
    tiles = [(i % NZ, i // NZ, i % 2, i // 2) for i in range(2 * ncol)]
    used = tiles[-1][1] + 1
    for zz, w, h, c in tiles:
        cols = slice(c * 128, (c + 1) * 128)
        q = grad[pl.ds(pl.multiple_of(dp * part + h * 16, 16), 16), cols]
        for s in range(n_dp - 1):
            q = q + yrecv[s, h * 16 : (h + 1) * 16, cols].astype(F32)
        t1[zz, w] = q.astype(BF16)
    for i in range(2 * ncol, used * NZ):
        t1[i % NZ, i // NZ] = jnp.zeros((16, 128), BF16)
    r1[used:] = jnp.zeros((ROW - used, NZ, 16, 128), BF16)

    head = pl.ds(0, used)
    for s in range(1, NZ):
        to = lax.rem(z + s, NZ)
        copy_to(t1.at[to], r1.at[head, z], g_s.at[0], g_r.at[0], zdev(s)).start()
    pltpu.make_async_copy(t1.at[z], r1.at[head, z], g_r.at[0]).start()

    rs_step(2)
    ret_start(1)

    wait_bytes(r1.at[head], g_r.at[0])
    for s in range(1, ROW):
        to = lax.rem(j + s, ROW)
        copy_to(r1.at[to], r2.at[j], g_s.at[1], g_r.at[1], rowdev(to)).start()
    pltpu.make_async_copy(r1.at[j], r2.at[j], g_r.at[1]).start()

    rs_step(3)
    ret_start(0)

    wait_bytes(r2, g_r.at[1])
    n = ROW * NZ
    r2f[...] = r2[...].reshape(n * 16, 128).astype(F32)
    for t in range(16):
        rows = pl.ds(t, n, stride=16)
        r2f[rows, :] = dot(pmat[...], r2f[rows, :].astype(BF16))
    s2 = r2f[...].astype(BF16).reshape(ROW, NZ, 16, 128)
    r2[...] = s2
    for s in range(1, ROW):
        to = lax.rem(j + s, ROW)
        copy_to(r2.at[to], rb2.at[j], g_s.at[2], g_r.at[2], rowdev(to)).start()
    pltpu.make_async_copy(r2.at[j], rb2.at[j], g_r.at[2]).start()

    rs_step(4)

    wait_bytes(rb2, g_r.at[2])
    for s in range(1, NZ):
        to = lax.rem(z + s, NZ)
        copy_to(rb2.at[head, to], rb1.at[z], g_s.at[3], g_r.at[3], zdev(s)).start()
    pltpu.make_async_copy(rb2.at[head, z], rb1.at[z], g_r.at[3]).start()

    def keep(cols, v):
        mix[:, cols] = v

    partial(0, keep)

    wait_bytes(rb1, g_r.at[3])
    for zz, w, h, c in tiles:
        yq[h * 16 : (h + 1) * 16, c * 128 : (c + 1) * 128] = rb1[zz, w]
    for s in range(1, n_dp):
        to = lax.rem(dp + s, n_dp)
        copy_to(yq, yo.at[ds(dp, part)], y_s.at[1], y_r.at[1], dpdev(to)).start()
    pltpu.make_async_copy(yq, yo.at[ds(dp, part)], y_r.at[1]).start()

    rs_copy(RIGHT, 4).wait_recv()
    rs_copy(LEFT, 4).wait_recv()

    def final(i, carry):
        cols = ds(i, CT)
        v = mix[:, cols] + rsr[0, 3, :, cols].astype(F32) + rsr[1, 3, :, cols].astype(F32)
        outs[0, :, cols] = v.astype(BF16)
        return carry

    row_sent(outs.at[0], rt_s.at[0])
    lax.fori_loop(0, width // CT, final, 0)
    stores = [pltpu.make_async_copy(outs.at[0], mixed_out, st.at[0])]
    stores[0].start()
    wait_bytes(yo, y_r.at[1])
    stores.append(pltpu.make_async_copy(yo, grads_out, st.at[1]))
    stores[1].start()

    for a in (0, 1):
        for k in range(1, NZ // 2 + 1):
            ring_copy(a, RIGHT, k).wait_send()
            ring_copy(a, LEFT, k).wait_send()
    for c in metas.values():
        c.wait_send()
    for p in range(NZ):
        row_sent(xs.at[1, p], x_s.at[1, p])
        if p > 0:
            row_sent(outs.at[p], rt_s.at[p])
    for way in (RIGHT, LEFT):
        for k in range(1, NZ // 2 + 1):
            rs_copy(way, k).wait_send()
    wait_bytes(yrecv, y_s.at[0])
    wait_bytes(yo.at[pl.ds(0, (n_dp - 1) * part)], y_s.at[1])
    wait_bytes(rb1.at[pl.ds(0, NZ - 1)], g_s.at[0])
    wait_bytes(r2.at[pl.ds(0, ROW - 1)], g_s.at[1])
    wait_bytes(r2.at[pl.ds(0, ROW - 1)], g_s.at[2])
    wait_bytes(rb1.at[pl.ds(0, NZ - 1)], g_s.at[3])
    for c in stores:
        c.wait()


def body(tokens, cotangent, routing, weights, choice, table, gate_up, down, amap, bmap):
    n_dp = lax.axis_size("dp")
    tok, width = tokens.shape
    rank, ff = bmap.shape[2:]
    rank2 = 2 * rank
    src, wgt = route_meta(routing, weights, choice, table)
    meta = jnp.concatenate(
        [src.reshape(NZ, 1, BLK), wgt.reshape(NZ, 1, BLK), jnp.zeros((NZ, 6, BLK), F32)], axis=1
    )
    order = table.reshape(NZ, ROW).T.reshape(-1)
    pmat = (order[:, None] == order[None, :]).astype(BF16)
    gcols = width + ff
    part = rank2 // n_dp
    used = (2 * gcols // 128 + NZ - 1) // NZ
    hbm = pl.BlockSpec(memory_space=pl.ANY)
    vmem = pl.BlockSpec(memory_space=pltpu.VMEM)
    V = pltpu.VMEM
    S = pltpu.SemaphoreType.DMA
    mixed, grads = pl.pallas_call(
        kernel,
        out_shape=(
            jax.ShapeDtypeStruct((tok, width), BF16),
            jax.ShapeDtypeStruct((rank2, gcols), BF16),
        ),
        in_specs=[hbm, hbm, vmem, vmem, hbm, hbm, hbm, hbm],
        out_specs=(hbm, hbm),
        scratch_shapes=[
            V((2, NZ, BLK, width), BF16),
            V((NZ, 8, BLK), F32),
            V((NZ, BLK, BLK), BF16),
            V((NZ, BLK, BLK), F32),
            V((2, NZ, BLK, width), BF16),
            V((2, NZ, BLK, width), BF16),
            V((NZ, BLK, width), BF16),
            V((NZ, BLK, width), BF16),
            V((2, NZ // 2, BLK, width), BF16),
            V((BLK, width), F32),
            V((width, 2 * ff), BF16),
            V((ff, width), BF16),
            V((width, rank2), BF16),
            V((2, rank2, ff), BF16),
            V((NZ * BLK, rank2), BF16),
            V((NZ * BLK, ff), F32),
            V((NZ * BLK, ff), F32),
            V((256, ff), BF16),
            V((rank2, gcols), F32),
            V((rank2, gcols), BF16),
            V((n_dp - 1, part, gcols), BF16),
            V((NZ, used, 16, 128), BF16),
            V((ROW, NZ, 16, 128), BF16),
            V((ROW, NZ, 16, 128), BF16),
            V((ROW * NZ * 16, 128), F32),
            V((ROW, NZ, 16, 128), BF16),
            V((NZ, used, 16, 128), BF16),
            V((part, gcols), BF16),
            V((rank2, gcols), BF16),
            S((7,)),
            S((2, 2, NZ // 2)),
            S((2, 2, NZ // 2)),
            S((NZ,)),
            S((NZ,)),
            S((2, NZ)),
            S((2, NZ)),
            S((NZ,)),
            S((NZ,)),
            S((2, NZ // 2)),
            S((2, NZ // 2)),
            S((2,)),
            S((2,)),
            S((4,)),
            S((4,)),
            S((2,)),
        ],
        compiler_params=pltpu.CompilerParams(
            collective_id=0, has_side_effects=True, vmem_limit_bytes=62 * 2**20
        ),
        cost_estimate=pl.CostEstimate(
            flops=16 * 10**9, bytes_accessed=14 * 2**20, transcendentals=NZ * BLK * ff
        ),
        name="moe_step",
    )(tokens, cotangent, meta, pmat, gate_up[0], down[0], amap[0], bmap[0])
    grad_a = grads[:, :width].astype(F32).T
    grad_b = grads[:, width:].astype(F32).reshape(1, 2, rank, ff)
    return mixed, grad_a[None], grad_b


def solution(mesh):
    both = P(("dp", "expert"), None)
    return jax.shard_map(
        body,
        mesh=mesh,
        in_specs=(both, both, both, both, both, P(), P("expert", None, None), P("expert", None, None),
                  P("expert", None, None), P("expert", None, None, None)),
        out_specs=(both, P("expert", None, None), P("expert", None, None, None)),
        check_vma=False,
    )
```

time: 440 us -> 217 us (0.49)
  waiting for transfers between devices: 283 us -> 0 us
  Pallas kernels: 0 us -> 198 us
  matrix products: 60.7 us -> 5.98 us
  starting transfers between devices: 31.9 us -> 0 us
  blocking collectives: 26.7 us -> 0 us
  between operations: 14.2 us -> 0.71 us
  local copies, waits for them, and re-layouts: 15.9 us -> 7.03 us
    all_to_all x4 -> x0, waiting for transfers between devices: 228 us -> none  [exchange(): return lax.all_to_all(v, 'expert', split_axis=0, concat_axis=0, tiled=True)]
    pallas_call x0 -> x1, Pallas kernels: none -> 198 us  [body(): pl.pallas_call(kernel, out_shape=(jax.ShapeDtypeStruct((tok, width), BF16...]
    dot_general x17 -> x1, matrix products: 60.7 us -> 5.98 us  [route_meta(): ahead = jnp.dot(tri, picked.astype(BF16), preferred_element_type=F32)]
    all_to_all x4 -> x0, starting transfers between devices: 31.6 us -> none  [exchange(): return lax.all_to_all(v, 'expert', split_axis=0, concat_axis=0, tiled=True)]
    all_gather x1 -> x0, waiting for transfers between devices: 29.7 us -> none  [body(): full = lax.all_gather(mine, 'dp', axis=0, tiled=True)]
    all_to_all x1 -> x0, blocking collectives: 26.7 us -> none  [exchange(): return lax.all_to_all(v, 'expert', split_axis=0, concat_axis=0, tiled=True)]
    reduce_scatter x1 -> x0, waiting for transfers between devices: 24.1 us -> none  [body(): part = lax.psum_scatter(grads, 'dp', scatter_dimension=0, tiled=True)]
    unnamed x20 -> x7, local copies, waits for them, and re-layouts: 10.5 us -> 4.47 us
  transfers between devices with their start and end apart: 6 -> 0, of which waited for: 6 -> 0; matrix products, arithmetic and copies ran while one was open for 9% -> 0% of each run, Pallas kernels for 0% -> 0%
where the time goes in v2:
time: 217 us; the launch traced here: 216 us
  Pallas kernels  198 us (91%)
  local copies, waits for them, and re-layouts  7.03 us (3%)
  matrix products  5.98 us (3%)
  other arithmetic  5.13 us (2%)
    pallas_call x1, Pallas kernels, body(): pl.pallas_call(kernel, out_shape=(jax.ShapeDtypeStruct((tok, width), BF16...  198 us
    dot_general x1, matrix products, route_meta(): ahead = jnp.dot(tri, picked.astype(BF16), preferred_element_type=F32)  5.98 us
    unnamed x7, local copies, waits for them, and re-layouts  4.47 us

profile of v2, /device:TPU:1, one launch (start us, length us, event | category | flops | bytes accessed | tf_op | source)
XLA Modules:
  0.0 216.4 jit_solution(1719476585476378079)
XLA Ops:
  0.6 0.1 pad.2.clone
  0.7 0.9 fusion.16
  1.7 0.7 reshape.57
  2.4 0.1 copy.31
  2.5 0.1 eq.89
  2.5 0.7 compare_convert_fusion.1.pmat
  3.2 0.8 copy.24
  4.0 0.1 eq.76
  4.1 0.8 copy.27
  4.9 0.1 broadcast_in_dim.51
  5.0 0.8 copy.25
  5.8 0.1 rem.30
  5.9 6.0 %fusion.1 = f32[1024,64]{0,1:T(8,128)S(1)} fusion(s32[64]{0:T(128)S(1)} %get-tuple-element.19, s32[64]{0:T(128)S(1)} %compare_select_fusion, s32[1024]{0:T(1024)S(1)} %rem.30, s32[1024]{0:T(1024)S(1)} %eq.76, s32[64]{0:T(128)} %param.15, pred[64]{0:T(512)(128)(4,1)S(1)} %broadcast_compare_fusion), kind=kOutput, calls=%fused_computation.5 | convolution fusion | flops 136642560 | bytes 271168 | tf_op jit(solution)/shard_map/dot_general | solution.py:33
  11.9 0.9 select_reduce_fusion.1
  12.8 0.1 copy.28
  12.9 0.1 reshape.56
  12.9 0.1 copy.26
  13.0 0.1 reshape.55
  13.1 0.7 maximum_maximum_fusion.meta
  13.8 197.6 %moe_step.1 = (bf16[128,2048]{1,0:T(8,128)(2,1)}, bf16[128,2816]{1,0:T(8,128)(2,1)}) custom-call(bf16[128,2048]{1,0:T(8,128)(2,1)} %tokens.1, bf16[128,2048]{1,0:T(8,128)(2,1)} %cots.1, f32[8,8,128]{2,1,0:T(8,128)} %maximum_maximum_fusion.meta, bf16[64,64]{1,0:T(8,128)(2,1)} %compare_convert_fusion.1.pmat, bf16[2048,1536]{1,0:T(8,128)(2,1)} %bitcast.21, ...), custom_call_target="tpu_custom_call" | custom-call | flops 16000000000 | bytes 14680064 | tf_op jit(solution)/shard_map/moe_step/pallas_call | solution.py:474
  211.4 0.0 copy-start
  211.4 1.0 slice.7
  212.4 0.8 convert.3
  213.2 1.1 convert_bitcast_fusion
  214.3 1.3 copy.32
  215.7 0.0 copy-done
  215.7 0.8 copy.34
  (5 shorter events, 0.0 us)
Async XLA Ops:
  211.4 4.2 %copy-start = (bf16[128,2048]{1,0:T(8,128)(2,1)S(1)}, bf16[128,2048]{1,0:T(8,128)(2,1)}, u32[]{:S(2)}) copy-start(bf16[128,2048]{1,0:T(8,128)(2,1)} %get-tuple-element.23) | copy-start | bytes 1572868

commit v3 on v2

v3 whole, which is shorter than its diff:
```python
import jax
import jax.numpy as jnp
from jax import lax
from jax.experimental import pallas as pl
from jax.experimental.pallas import tpu as pltpu
from jax.sharding import PartitionSpec as P

ADAPTER_SCALE = 0.5
CAP = 16
ROW = 8
NZ = 8
BLK = 128
F32 = jnp.float32
BF16 = jnp.bfloat16
MESH = pl.DeviceIdType.MESH
RIGHT, LEFT = 0, 1


def dot(a, b):
    return jnp.dot(a, b, preferred_element_type=F32)


def dot_t(a, b):
    return lax.dot_general(a, b, (((1,), (1,)), ((), ())), preferred_element_type=F32)


def t_dot(a, b):
    return lax.dot_general(a, b, (((0,), (0,)), ((), ())), preferred_element_type=F32)


def ds(i, n):
    return pl.ds(pl.multiple_of(i * n, n), n)


def kernel(
    tokens, cots, routing, weights, choice, table, gate_up, down, amap, bmap,
    mixed_out, grad_a_out, grad_b_out,
    ring, meta, metar, pick, wcol, whl, xs, xr, outs, rets, rsr,
    gu, dn, am, bm, low, act, mul, hid, grad,
    ysend, yrecv, t1, r1, r2, r2f, rb2, rb1, yq, yo,
    ld, ag_s, ag_r, mt_s, mt_r, x_s, x_r, rt_s, rt_r, rs_s, rs_r, y_s, y_r, g_s, g_r, w_s, st,
):
    width = tokens.shape[1]
    ff = dn.shape[0]
    rank2 = am.shape[1]
    n_dp = yrecv.shape[0] + 1
    part = rank2 // n_dp
    dp = lax.axis_index("dp")
    e = lax.axis_index("expert")
    z, j = e // ROW, e % ROW

    def zdev(step):
        return (dp, lax.rem(z + step + NZ, NZ) * ROW + j)

    def rowdev(i):
        return (dp, z * ROW + i)

    def dpdev(i):
        return (i, e)

    bar = pltpu.get_barrier_semaphore()
    for s in range(1, NZ):
        pl.semaphore_signal(bar, inc=1, device_id=zdev(s), device_id_type=MESH)
    for s in range(1, ROW):
        pl.semaphore_signal(bar, inc=1, device_id=rowdev(lax.rem(j + s, ROW)), device_id_type=MESH)
    for s in range(1, n_dp):
        pl.semaphore_signal(bar, inc=1, device_id=dpdev(lax.rem(dp + s, n_dp)), device_id_type=MESH)

    rh = rank2 // 2
    loads = [
        pltpu.make_async_copy(tokens, ring.at[0, 0], ld.at[0]),
        pltpu.make_async_copy(cots, ring.at[1, 0], ld.at[1]),
        pltpu.make_async_copy(gate_up, gu, ld.at[2]),
        pltpu.make_async_copy(down, dn, ld.at[3]),
        pltpu.make_async_copy(amap, am, ld.at[4]),
        pltpu.make_async_copy(bmap.at[0], bm.at[0, pl.ds(0, rh)], ld.at[5]),
        pltpu.make_async_copy(bmap.at[1], bm.at[1, pl.ds(rh, rh)], ld.at[6]),
    ]
    for c in loads:
        c.start()
    bm[0, rh:, :] = jnp.zeros((rh, ff), BF16)
    bm[1, :rh, :] = jnp.zeros((rh, ff), BF16)

    slots = table.shape[1]
    top = routing.shape[0]
    trow = jnp.concatenate([table[...].astype(F32)] * (BLK // slots), axis=1)
    tcol = jnp.broadcast_to(trow, (BLK, BLK)).T[:slots]
    same = (tcol == trow).astype(F32)
    sub = lax.broadcasted_iota(jnp.int32, (slots, BLK), 0)
    lane = lax.broadcasted_iota(jnp.int32, (slots, BLK), 1)
    cnt = jnp.sum(jnp.where(lane < slots, same, 0.0), axis=1, keepdims=True)
    occ = jnp.sum(jnp.where(lane < sub, same, 0.0), axis=1, keepdims=True)
    picked = jnp.zeros((slots, BLK), F32)
    wsum = jnp.zeros((slots, BLK), F32)
    for k in range(top):
        want = choice[k : k + 1, :].astype(F32)
        want = want - cnt * jnp.floor((want + 0.5) / cnt)
        hit = (tcol == routing[k : k + 1, :].astype(F32)) & (want == occ)
        picked = jnp.where(hit, 1.0, picked)
        wsum = jnp.where(hit, weights[k : k + 1, :], wsum)
    tri = lax.broadcasted_iota(jnp.int32, (BLK, BLK), 0) < lax.broadcasted_iota(jnp.int32, (BLK, BLK), 1)
    ahead = dot(picked.astype(BF16), tri.astype(F32).astype(BF16))
    rank = jnp.where(picked > 0.0, ahead, -1.0)
    for i in range(NZ):
        meta[i, :ROW] = rank[i * ROW : (i + 1) * ROW]
        meta[i, ROW:] = wsum[i * ROW : (i + 1) * ROW]
    metar[0] = meta[z]
    pl.semaphore_wait(bar, NZ - 1 + ROW - 1 + n_dp - 1)

    def copy_to(src, dst, send, recv, device):
        return pltpu.make_async_remote_copy(
            src_ref=src, dst_ref=dst, send_sem=send, recv_sem=recv, device_id=device, device_id_type=MESH
        )

    def wait_bytes(ref, sem):
        pltpu.make_async_copy(ref, ref, sem).wait()

    HW = width // 2

    def half(h):
        return pl.ds(h * HW, HW)

    def ring_copy(a, way, k, h):
        if way == RIGHT:
            frm, to, dev = (0 if k == 1 else 2 * k - 3), 2 * k - 1, zdev(1)
        else:
            frm, to, dev = 2 * k - 2, min(2 * k, NZ - 1), zdev(-1)
        rows = pl.ds(0, BLK)
        if k == NZ // 2:
            rows = pl.ds(0 if way == RIGHT else BLK // 2, BLK // 2)
        src, dst = ring.at[a, frm, rows, half(h)], ring.at[a, to, rows, half(h)]
        return copy_to(src, dst, ag_s.at[a, way, k - 1, h], ag_r.at[a, way, k - 1, h], dev)

    def ring_start(a, k, h):
        ring_copy(a, RIGHT, k, h).start()
        ring_copy(a, LEFT, k, h).start()

    loads[0].wait()
    ring_start(0, 1, 0)
    ring_start(0, 1, 1)

    def meta_copy(s):
        place = 2 * s - 1 if s <= NZ // 2 else 2 * (NZ - s)
        dst_row = lax.rem(z + s, NZ)
        return place, copy_to(meta.at[dst_row], metar.at[place], mt_s.at[place], mt_r.at[place], zdev(s))

    metas = dict(meta_copy(s) for s in range(1, NZ))
    for c in metas.values():
        c.start()

    def prepare(p):
        order = lax.broadcasted_iota(jnp.int32, (CAP, BLK), 0).astype(F32)
        parts = []
        for i in range(ROW):
            rows = slice(i * CAP, (i + 1) * CAP)
            hit = jnp.broadcast_to(metar[p, i : i + 1, :], (CAP, BLK)) == order
            pick[p, rows] = jnp.where(hit, 1.0, 0.0).astype(BF16)
            w = jnp.where(hit, jnp.broadcast_to(metar[p, ROW + i : ROW + i + 1, :], (CAP, BLK)), 0.0)
            wcol[p, rows] = jnp.broadcast_to(jnp.sum(w, axis=1, keepdims=True), (CAP, BLK))
            parts.append(w)
        wt = jnp.concatenate(parts, axis=0).T
        hi = wt.astype(BF16)
        whl[p, 0] = hi
        whl[p, 1] = (wt - hi.astype(F32)).astype(BF16)

    CT = 512

    def relay(a, p, h):
        def tile(i, carry):
            cols = pl.ds(pl.multiple_of(h * HW + i * CT, CT), CT)
            v = dot(pick[p], ring[a, p, :, cols])
            if a == 1:
                v = v * wcol[p][:, 0:1]
            xs[a, p, :, cols] = v.astype(BF16)
            return carry

        lax.fori_loop(0, HW // CT, tile, 0)
        row_send(xs.at[a, p, :, half(h)], xr.at[a, p, :, half(h)], x_s.at[a, p, h], x_r.at[a, p, h])

    def rows_here(a, p):
        for h in (0, 1):
            wait_bytes(xr.at[a, p, :, half(h)], x_r.at[a, p, h])

    def rows_gone(a, p):
        for h in (0, 1):
            row_sent(xs.at[a, p, :, half(h)], x_s.at[a, p, h])

    def row_send(src, dst, send, recv):
        mine = ds(j, CAP)
        for s in range(1, ROW):
            to = lax.rem(j + s, ROW)
            copy_to(src.at[ds(to, CAP)], dst.at[mine], send, recv, rowdev(to)).start()
        pltpu.make_async_copy(src.at[mine], dst.at[mine], recv).start()

    def row_sent(src, send):
        wait_bytes(src.at[pl.ds(0, (ROW - 1) * CAP)], send)

    FT = 256
    CH = 256

    def forward(c):
        for p in (2 * c, 2 * c + 1):
            rows_here(0, p)
        rows = pl.ds(c * CH, CH)
        x = xr.at[0, pl.ds(2 * c, 2)]

        def xv():
            return x[...].reshape(CH, width)

        low[rows, :] = dot(xv(), am[...]).astype(BF16)

        def tile(f, carry):
            cols = ds(f, FT)
            up_cols = pl.ds(pl.multiple_of(ff + f * FT, FT), FT)
            lw = low[rows, :]
            pg = dot(xv(), gu[:, cols]) + ADAPTER_SCALE * dot(lw, bm[0, :, cols])
            pu = dot(xv(), gu[:, up_cols]) + ADAPTER_SCALE * dot(lw, bm[1, :, cols])
            sig = jax.nn.sigmoid(pg)
            ac = pg * sig
            act[rows, cols] = ac
            mul[rows, cols] = pu * (sig * (1.0 + pg * (1.0 - sig)))
            hid[:, cols] = (ac * pu).astype(BF16)
            return carry

        lax.fori_loop(0, ff // FT, tile, 0)

        def otile(i, carry):
            cols = ds(i, CT)
            o = dot(hid[...], dn[:, cols]).astype(BF16)
            outs[2 * c, :, cols] = o[:BLK]
            outs[2 * c + 1, :, cols] = o[BLK:]
            return carry

        lax.fori_loop(0, width // CT, otile, 0)

    def backward(c):
        for p in (2 * c, 2 * c + 1):
            rows_here(1, p)
        rows = pl.ds(c * CH, CH)

        def tile(f, lg):
            cols = ds(f, FT)
            gcols = pl.ds(pl.multiple_of(width + f * FT, FT), FT)
            back = dot_t(xr[1, pl.ds(2 * c, 2)].reshape(CH, width), dn[cols, :])
            g_up = (back * act[rows, cols]).astype(BF16)
            g_gate = (back * mul[rows, cols]).astype(BF16)
            lw = low[rows, :]
            gb0 = ADAPTER_SCALE * t_dot(lw, g_gate)
            gb1 = ADAPTER_SCALE * t_dot(lw, g_up)
            gb = jnp.concatenate([gb0[:rh], gb1[rh:]], axis=0)
            if c == 0:
                grad[:, gcols] = gb
            else:
                grad[:, gcols] += gb
            return lg + dot_t(g_gate, bm[0, :, cols]) + dot_t(g_up, bm[1, :, cols])

        lg = lax.fori_loop(0, ff // FT, tile, jnp.zeros((CH, rank2), F32))
        lgb = (ADAPTER_SCALE * lg).astype(BF16)

        def gtile(i, carry):
            cols = ds(i, CT)
            ga = t_dot(lgb, xr[0, pl.ds(2 * c, 2), :, cols].reshape(CH, CT))
            if c == 0:
                grad[:, cols] = ga
            else:
                grad[:, cols] += ga
            return carry

        lax.fori_loop(0, width // CT, gtile, 0)

    def places(k):
        return (0,) if k == 0 else (7,) if k == NZ // 2 else (2 * k - 1, 2 * k)

    prepare(0)
    for h in (0, 1):
        relay(0, 0, h)
    loads[1].wait()
    for h in (0, 1):
        relay(1, 0, h)
    for a in (0, 1):
        for k in range(1, NZ // 2 + 1):
            for h in (0, 1):
                ring_copy(a, RIGHT, k, h).wait_recv()
                ring_copy(a, LEFT, k, h).wait_recv()
                if k < NZ // 2:
                    ring_start(a, k + 1, h)
                if a == 0 and k == NZ // 2 - 1 and h == 1:
                    ring_start(1, 1, 0)
                    ring_start(1, 1, 1)
                for p in places(k):
                    if a == 0 and h == 0:
                        metas[p].wait_recv()
                        prepare(p)
                    relay(a, p, h)
            if a == 0 and k == 1:
                for c in loads[2:]:
                    c.wait()
            if a == 0 and k >= 2:
                forward(k - 2)
            if a == 1 and k == 1:
                forward(3)
            if a == 1 and k in (2, 3):
                backward(k - 2)

    groups = [(h, k) for k in range(NZ // 2, -1, -1) for h in (0, 1)]

    def ret_refs(h, p):
        return outs.at[p, :, half(h)], rets.at[p, :, half(h)], rt_s.at[h, p], rt_r.at[h, p]

    def ret_start(g):
        if g >= len(groups):
            return
        h, k = groups[g]
        for p in places(k):
            row_send(*ret_refs(h, p))

    GP = grad.shape[1] // 2
    NT = 2 * GP // 128
    WT = (NT + NZ - 1) // NZ

    def piece(q):
        return pl.ds(q * GP, GP)

    def dp_send(q):
        ysend[:, piece(q)] = grad[:, piece(q)].astype(BF16)
        for s in range(1, n_dp):
            to = lax.rem(dp + s, n_dp)
            copy_to(
                ysend.at[ds(to, part), piece(q)], yrecv.at[s - 1, :, piece(q)], y_s.at[0, q], y_r.at[0, q], dpdev(to)
            ).start()

    def tiles(q):
        return [(i % NZ, q * WT + i // NZ, i % 2, q * (NT // 2) + i // 2) for i in range(NT)]

    def owners(q):
        return pl.ds(q * WT, WT)

    def z_send(q):
        wait_bytes(yrecv.at[:, :, piece(q)], y_r.at[0, q])
        for zz, w, hh, c in tiles(q):
            cols = slice(c * 128, (c + 1) * 128)
            v = grad[pl.ds(pl.multiple_of(dp * part + hh * 16, 16), 16), cols]
            for s in range(n_dp - 1):
                v = v + yrecv[s, hh * 16 : (hh + 1) * 16, cols].astype(F32)
            t1[zz, w] = v.astype(BF16)
        for i in range(NT, WT * NZ):
            t1[i % NZ, q * WT + i // NZ] = jnp.zeros((16, 128), BF16)
        for s in range(1, NZ):
            to = lax.rem(z + s, NZ)
            copy_to(t1.at[to, owners(q)], r1.at[owners(q), z], g_s.at[0, q], g_r.at[0, q], zdev(s)).start()
        pltpu.make_async_copy(t1.at[z, owners(q)], r1.at[owners(q), z], g_r.at[0, q]).start()

    def row_copy(w):
        return copy_to(r1.at[w], r2.at[:, j], w_s.at[w], g_r.at[1, 0], rowdev(w))

    def x_send(q):
        wait_bytes(r1.at[owners(q)], g_r.at[0, q])
        for w in range(q * WT, (q + 1) * WT):

            @pl.when(j != w)
            def _(w=w):
                row_copy(w).start()

            @pl.when(j == w)
            def _(w=w):
                pltpu.make_async_copy(r1.at[w], r2.at[:, j], g_r.at[1, 0]).start()

    def owner(q):
        return (j >= q * WT) & (j < (q + 1) * WT)

    def x_sum(q):
        @pl.when(owner(q))
        def _():
            wait_bytes(r2, g_r.at[1, 0])
            pm = same[:, :slots].astype(BF16)
            r2f[...] = r2[...].reshape(slots * 16, 128).astype(F32)
            for t in range(16):
                rows = pl.ds(t, slots, stride=16)
                r2f[rows, :] = dot(pm, r2f[rows, :].astype(BF16))
            r2[...] = r2f[...].astype(BF16).reshape(NZ, ROW, 16, 128)
            for s in range(1, ROW):
                to = lax.rem(j + s, ROW)
                copy_to(r2.at[:, to], rb2.at[j], g_s.at[1, 0], g_r.at[2, q], rowdev(to)).start()
            pltpu.make_async_copy(r2.at[:, j], rb2.at[j], g_r.at[2, q]).start()

    def z_back(q):
        wait_bytes(rb2.at[owners(q)], g_r.at[2, q])
        for s in range(1, NZ):
            to = lax.rem(z + s, NZ)
            copy_to(rb2.at[owners(q), to], rb1.at[z, owners(q)], g_s.at[2, q], g_r.at[3, q], zdev(s)).start()
        pltpu.make_async_copy(rb2.at[owners(q), z], rb1.at[z, owners(q)], g_r.at[3, q]).start()

    def dp_back(q):
        wait_bytes(rb1.at[:, owners(q)], g_r.at[3, q])
        for zz, w, hh, c in tiles(q):
            yq[hh * 16 : (hh + 1) * 16, c * 128 : (c + 1) * 128] = rb1[zz, w]
        dst = yo.at[ds(dp, part), piece(q)]
        for s in range(1, n_dp):
            to = lax.rem(dp + s, n_dp)
            copy_to(yq.at[:, piece(q)], dst, y_s.at[1, q], y_r.at[1, q], dpdev(to)).start()
        pltpu.make_async_copy(yq.at[:, piece(q)], dst, y_r.at[1, q]).start()

    def turn(first, last):
        def block(i, carry):
            am[ds(i, BLK), :] = yo[:, ds(i, BLK)].astype(F32).T.astype(BF16)
            return carry

        lax.fori_loop(first, last, block, 0)

    def partial(h, p, store):
        _, dst, _, recv = ret_refs(h, p)
        wait_bytes(dst, recv)

        def tile(i, carry):
            cols = pl.ds(pl.multiple_of(h * HW + i * CT, CT), CT)
            r = rets[p, :, cols]
            store(cols, dot(whl[p, 0], r) + dot(whl[p, 1], r))
            return carry

        lax.fori_loop(0, HW // CT, tile, 0)

    def rs_copy(h, way, k):
        if k == 1:
            rows = pl.ds(0 if way == RIGHT else BLK // 2, BLK // 2)
            src, dst = xs.at[0, 7, rows, half(h)], rsr.at[way, 0, rows, half(h)]
        else:
            p = 2 * (NZ // 2 + 1 - k) - (0 if way == RIGHT else 1)
            src, dst = xs.at[0, p, :, half(h)], rsr.at[way, k - 1, :, half(h)]
        return copy_to(src, dst, rs_s.at[h, way, k - 1], rs_r.at[h, way, k - 1], zdev(1 if way == RIGHT else -1))

    def rs_step(h, k):
        if k == 1:

            def store(cols, v):
                xs[0, 7, :, cols] = v.astype(BF16)

            partial(h, 7, store)
            for way in (RIGHT, LEFT):
                rs_copy(h, way, 1).start()
            return
        for way in (RIGHT, LEFT):
            p = 2 * (NZ // 2 + 1 - k) - (0 if way == RIGHT else 1)
            rs_copy(h, way, k - 1).wait_recv()

            def store(cols, v, p=p, way=way):
                if k == 2:
                    m = BLK // 2
                    mine = slice(0, m) if way == RIGHT else slice(m, BLK)
                    rest = slice(m, BLK) if way == RIGHT else slice(0, m)
                    xs[0, p, mine, cols] = (v[mine] + rsr[way, 0, mine, cols].astype(F32)).astype(BF16)
                    xs[0, p, rest, cols] = v[rest].astype(BF16)
                else:
                    xs[0, p, :, cols] = (v + rsr[way, k - 2, :, cols].astype(F32)).astype(BF16)

            partial(h, p, store)
            rs_copy(h, way, k).start()

    def rs_last(h):
        for way in (RIGHT, LEFT):
            rs_copy(h, way, NZ // 2).wait_recv()
        src, _, send, _ = ret_refs(h, 0)
        row_sent(src, send)

        def store(cols, v):
            v = v + rsr[0, 3, :, cols].astype(F32) + rsr[1, 3, :, cols].astype(F32)
            outs[0, :, cols] = v.astype(BF16)

        partial(h, 0, store)
        c = pltpu.make_async_copy(outs.at[0, :, half(h)], mixed_out.at[:, half(h)], st.at[h])
        c.start()
        stores.append(c)

    stores = []

    def store_out(src, dst, i):
        c = pltpu.make_async_copy(src, dst, st.at[i])
        c.start()
        stores.append(c)

    for g in range(3):
        ret_start(g)
    backward(2)
    rows_gone(0, 7)
    rs_step(0, 1)
    backward(3)
    dp_send(0)
    dp_send(1)
    rs_step(1, 1)
    ret_start(3)
    for p in range(NZ - 1):
        rows_gone(0, p)
    rs_step(0, 2)
    ret_start(4)
    z_send(0)
    rs_step(1, 2)
    ret_start(5)
    z_send(1)
    x_send(0)
    rs_step(0, 3)
    ret_start(6)
    x_send(1)
    rs_step(1, 3)
    ret_start(7)
    x_sum(0)
    rs_step(0, 4)
    ret_start(8)
    ret_start(9)
    x_sum(1)
    z_back(0)
    rs_step(1, 4)
    z_back(1)
    dp_back(0)
    rs_last(0)
    rs_last(1)
    dp_back(1)
    cut = GP // BLK
    wait_bytes(yo.at[:, piece(0)], y_r.at[1, 0])
    turn(0, cut)
    wait_bytes(yo.at[:, piece(1)], y_r.at[1, 1])
    store_out(yo.at[:, pl.ds(width, ff)], grad_b_out, 3)
    turn(cut, width // BLK)
    store_out(am, grad_a_out, 2)

    for a in (0, 1):
        for k in range(1, NZ // 2 + 1):
            for h in (0, 1):
                ring_copy(a, RIGHT, k, h).wait_send()
                ring_copy(a, LEFT, k, h).wait_send()
    for c in metas.values():
        c.wait_send()
    for p in range(NZ):
        rows_gone(1, p)
        for h in (0, 1):
            if p > 0:
                src, _, send, _ = ret_refs(h, p)
                row_sent(src, send)
    for h in (0, 1):
        for way in (RIGHT, LEFT):
            for k in range(1, NZ // 2 + 1):
                rs_copy(h, way, k).wait_send()
    for q in (0, 1):
        wait_bytes(yrecv.at[:, :, piece(q)], y_s.at[0, q])
        wait_bytes(yo.at[pl.ds(0, (n_dp - 1) * part), piece(q)], y_s.at[1, q])
        wait_bytes(rb1.at[pl.ds(0, NZ - 1), owners(q)], g_s.at[0, q])
        wait_bytes(rb1.at[pl.ds(0, NZ - 1), owners(q)], g_s.at[2, q])
        for w in range(q * WT, (q + 1) * WT):

            @pl.when(j != w)
            def _(w=w):
                row_copy(w).wait_send()

        @pl.when(owner(q))
        def _():
            wait_bytes(r1.at[pl.ds(0, ROW - 1)], g_s.at[1, 0])

    for c in stores:
        c.wait()


def body(tokens, cotangent, routing, weights, choice, table, gate_up, down, amap, bmap):
    n_dp = lax.axis_size("dp")
    tok, width = tokens.shape
    rank, ff = bmap.shape[2:]
    rank2 = 2 * rank
    gcols = width + ff
    part = rank2 // n_dp
    used = (2 * gcols // 128 + NZ - 1) // NZ
    hbm = pl.BlockSpec(memory_space=pl.ANY)
    vmem = pl.BlockSpec(memory_space=pltpu.VMEM)
    V = pltpu.VMEM
    S = pltpu.SemaphoreType.DMA
    mixed, grad_a, grad_b = pl.pallas_call(
        kernel,
        out_shape=(
            jax.ShapeDtypeStruct((tok, width), BF16),
            jax.ShapeDtypeStruct((width, rank2), BF16),
            jax.ShapeDtypeStruct((rank2, ff), BF16),
        ),
        in_specs=[hbm, hbm, vmem, vmem, vmem, vmem, hbm, hbm, hbm, hbm],
        out_specs=(hbm, hbm, hbm),
        scratch_shapes=[
            V((2, NZ, BLK, width), BF16),
            V((NZ, 2 * ROW, BLK), F32),
            V((NZ, 2 * ROW, BLK), F32),
            V((NZ, BLK, BLK), BF16),
            V((NZ, BLK, BLK), F32),
            V((NZ, 2, BLK, BLK), BF16),
            V((2, NZ, BLK, width), BF16),
            V((2, NZ, BLK, width), BF16),
            V((NZ, BLK, width), BF16),
            V((NZ, BLK, width), BF16),
            V((2, NZ // 2, BLK, width), BF16),
            V((width, 2 * ff), BF16),
            V((ff, width), BF16),
            V((width, rank2), BF16),
            V((2, rank2, ff), BF16),
            V((NZ * BLK, rank2), BF16),
            V((NZ * BLK, ff), F32),
            V((NZ * BLK, ff), F32),
            V((256, ff), BF16),
            V((rank2, gcols), F32),
            V((rank2, gcols), BF16),
            V((n_dp - 1, part, gcols), BF16),
            V((NZ, used, 16, 128), BF16),
            V((ROW, NZ, 16, 128), BF16),
            V((ROW, NZ, 16, 128), BF16),
            V((ROW * NZ * 16, 128), F32),
            V((ROW, NZ, 16, 128), BF16),
            V((NZ, used, 16, 128), BF16),
            V((part, gcols), BF16),
            V((rank2, gcols), BF16),
            S((7,)),
            S((2, 2, NZ // 2, 2)),
            S((2, 2, NZ // 2, 2)),
            S((NZ,)),
            S((NZ,)),
            S((2, NZ, 2)),
            S((2, NZ, 2)),
            S((2, NZ)),
            S((2, NZ)),
            S((2, 2, NZ // 2)),
            S((2, 2, NZ // 2)),
            S((2, 2)),
            S((2, 2)),
            S((3, 2)),
            S((4, 2)),
            S((used,)),
            S((4,)),
        ],
        compiler_params=pltpu.CompilerParams(
            collective_id=0, has_side_effects=True, vmem_limit_bytes=62 * 2**20
        ),
        cost_estimate=pl.CostEstimate(
            flops=16 * 10**9, bytes_accessed=14 * 2**20, transcendentals=NZ * BLK * ff
        ),
        name="moe_step",
    )(
        tokens, cotangent, routing.T, weights.T, choice.T, table.reshape(1, -1),
        gate_up[0], down[0], amap[0], bmap[0],
    )
    return mixed, grad_a.astype(F32)[None], grad_b.astype(F32).reshape(1, 2, rank, ff)


def solution(mesh):
    both = P(("dp", "expert"), None)
    return jax.shard_map(
        body,
        mesh=mesh,
        in_specs=(both, both, both, both, both, P(), P("expert", None, None), P("expert", None, None),
                  P("expert", None, None), P("expert", None, None, None)),
        out_specs=(both, P("expert", None, None), P("expert", None, None, None)),
        check_vma=False,
    )
```

time: 217 us -> 182 us (0.84)
  Pallas kernels: 198 us -> 174 us
  matrix products: 5.98 us -> 0 us
  local copies, waits for them, and re-layouts: 7.03 us -> 1.88 us
    pallas_call x1, Pallas kernels: 198 us -> 174 us  [body(): pl.pallas_call(kernel, out_shape=(jax.ShapeDtypeStruct((tok, width), BF16...]
    dot_general x1 -> x0, matrix products: 5.98 us -> none  [route_meta(): ahead = jnp.dot(tri, picked.astype(BF16), preferred_element_type=F32)]
    unnamed x7 -> x1, local copies, waits for them, and re-layouts: 4.47 us -> 1.88 us
where the time goes in v3:
time: 182 us; the launch traced here: 180 us
  Pallas kernels  174 us (96%)
  other arithmetic  3.78 us (2%)
  local copies, waits for them, and re-layouts  1.88 us (1%)
    pallas_call x1, Pallas kernels, body(): pl.pallas_call(kernel, out_shape=(jax.ShapeDtypeStruct((tok, width), BF16...  174 us

profile of v3, /device:TPU:1, one launch (start us, length us, event | category | flops | bytes accessed | tf_op | source)
XLA Modules:
  0.0 180.0 jit_solution(6311984374521807912)
XLA Ops:
  0.6 173.7 %moe_step.1 = (bf16[128,2048]{1,0:T(8,128)(2,1)}, bf16[2048,128]{1,0:T(8,128)(2,1)}, bf16[128,768]{1,0:T(8,128)(2,1)}) custom-call(bf16[128,2048]{1,0:T(8,128)(2,1)} %tokens.1, bf16[128,2048]{1,0:T(8,128)(2,1)} %cots.1, s32[8,128]{1,0:T(8,128)} %bitcast.18, f32[8,128]{1,0:T(8,128)} %bitcast.19, s32[8,128]{1,0:T(8,128)} %bitcast.20, s32[1,64]{1,0:T(1,128)} %bitcast.21, ...), custom_call_target="tpu_custom_call" | custom-call | flops 16000000000 | bytes 14680064 | tf_op jit(solution)/shard_map/moe_step/pallas_call | solution.py:572
  174.4 2.1 %bitcast_convert_fusion = f32[1,2048,128]{2,1,0:T(8,128)} fusion(bf16[2048,128]{1,0:T(8,128)(2,1)} %get-tuple-element.7), kind=kLoop, calls=%fused_computation | loop fusion | flops 262144 | bytes 1572864 | tf_op jit(solution)/shard_map/broadcast_in_dim | solution.py:641
  176.5 1.7 convert.3
  178.2 1.9 %copy.14 = bf16[128,2048]{1,0:T(8,128)(2,1)} copy(bf16[128,2048]{1,0:T(8,128)(2,1)} %get-tuple-element.12) | data formatting | bytes 1048576

commit v4 on v3

--- a/solution.py
+++ b/solution.py
@@ -233,34 +233,35 @@
 
         lax.fori_loop(0, width // CT, otile, 0)
 
-    def backward(c):
-        for p in (2 * c, 2 * c + 1):
+    def backward(first, n):
+        for p in range(first, first + n):
             rows_here(1, p)
-        rows = pl.ds(c * CH, CH)
+        nr = n * BLK
+        rows = pl.ds(first * BLK, nr)
 
         def tile(f, lg):
             cols = ds(f, FT)
             gcols = pl.ds(pl.multiple_of(width + f * FT, FT), FT)
-            back = dot_t(xr[1, pl.ds(2 * c, 2)].reshape(CH, width), dn[cols, :])
+            back = dot_t(xr[1, pl.ds(first, n)].reshape(nr, width), dn[cols, :])
             g_up = (back * act[rows, cols]).astype(BF16)
             g_gate = (back * mul[rows, cols]).astype(BF16)
             lw = low[rows, :]
             gb0 = ADAPTER_SCALE * t_dot(lw, g_gate)
             gb1 = ADAPTER_SCALE * t_dot(lw, g_up)
             gb = jnp.concatenate([gb0[:rh], gb1[rh:]], axis=0)
-            if c == 0:
+            if first == 0:
                 grad[:, gcols] = gb
             else:
                 grad[:, gcols] += gb
             return lg + dot_t(g_gate, bm[0, :, cols]) + dot_t(g_up, bm[1, :, cols])
 
-        lg = lax.fori_loop(0, ff // FT, tile, jnp.zeros((CH, rank2), F32))
+        lg = lax.fori_loop(0, ff // FT, tile, jnp.zeros((nr, rank2), F32))
         lgb = (ADAPTER_SCALE * lg).astype(BF16)
 
         def gtile(i, carry):
             cols = ds(i, CT)
-            ga = t_dot(lgb, xr[0, pl.ds(2 * c, 2), :, cols].reshape(CH, CT))
-            if c == 0:
+            ga = t_dot(lgb, xr[0, pl.ds(first, n), :, cols].reshape(nr, CT))
+            if first == 0:
                 grad[:, cols] = ga
             else:
                 grad[:, cols] += ga
@@ -299,8 +300,11 @@
                 forward(k - 2)
             if a == 1 and k == 1:
                 forward(3)
-            if a == 1 and k in (2, 3):
-                backward(k - 2)
+            if a == 1 and k == 2:
+                backward(0, 1)
+                backward(1, 2)
+            if a == 1 and k == 3:
+                backward(3, 2)
 
     groups = [(h, k) for k in range(NZ // 2, -1, -1) for h in (0, 1)]
 
@@ -477,49 +481,57 @@
         c.start()
         stores.append(c)
 
-    for g in range(3):
-        ret_start(g)
-    backward(2)
+    rows_gone(1, 5)
+    rows_gone(1, 6)
+    ret_start(0)
+    ret_start(1)
+    backward(5, 2)
+    rows_gone(1, 7)
+    ret_start(2)
+    backward(7, 1)
+    dp_send(0)
+    dp_send(1)
     rows_gone(0, 7)
     rs_step(0, 1)
-    backward(3)
-    dp_send(0)
-    dp_send(1)
     rs_step(1, 1)
     ret_start(3)
-    for p in range(NZ - 1):
-        rows_gone(0, p)
+    z_send(0)
+    rows_gone(0, 6)
+    rows_gone(0, 5)
     rs_step(0, 2)
-    ret_start(4)
-    z_send(0)
-    rs_step(1, 2)
-    ret_start(5)
     z_send(1)
     x_send(0)
+    ret_start(4)
+    x_send(1)
+    rs_step(1, 2)
+    x_sum(0)
+    ret_start(5)
+    x_sum(1)
+    rows_gone(0, 4)
+    rows_gone(0, 3)
     rs_step(0, 3)
     ret_start(6)
-    x_send(1)
+    z_back(0)
+    z_back(1)
     rs_step(1, 3)
     ret_start(7)
-    x_sum(0)
+    dp_back(0)
+    dp_back(1)
+    rows_gone(0, 2)
+    rows_gone(0, 1)
+    rows_gone(0, 0)
     rs_step(0, 4)
     ret_start(8)
     ret_start(9)
-    x_sum(1)
-    z_back(0)
     rs_step(1, 4)
-    z_back(1)
-    dp_back(0)
+    wait_bytes(yo.at[:, piece(0)], y_r.at[1, 0])
+    turn(0, GP // BLK)
+    wait_bytes(yo.at[:, piece(1)], y_r.at[1, 1])
+    store_out(yo.at[:, pl.ds(width, ff)], grad_b_out, 3)
+    turn(GP // BLK, width // BLK)
+    store_out(am, grad_a_out, 2)
     rs_last(0)
     rs_last(1)
-    dp_back(1)
-    cut = GP // BLK
-    wait_bytes(yo.at[:, piece(0)], y_r.at[1, 0])
-    turn(0, cut)
-    wait_bytes(yo.at[:, piece(1)], y_r.at[1, 1])
-    store_out(yo.at[:, pl.ds(width, ff)], grad_b_out, 3)
-    turn(cut, width // BLK)
-    store_out(am, grad_a_out, 2)
 
     for a in (0, 1):
         for k in range(1, NZ // 2 + 1):
@@ -529,7 +541,8 @@
     for c in metas.values():
         c.wait_send()
     for p in range(NZ):
-        rows_gone(1, p)
+        if p not in (5, 6, 7):
+            rows_gone(1, p)
         for h in (0, 1):
             if p > 0:
                 src, _, send, _ = ret_refs(h, p)

time: 182 us -> 175 us (0.962)
  Pallas kernels: 174 us -> 168 us
    pallas_call x1, Pallas kernels: 174 us -> 168 us  [body(): pl.pallas_call(kernel, out_shape=(jax.ShapeDtypeStruct((tok, width), BF16...]
where the time goes in v4:
time: 175 us; the launch traced here: 174 us
  Pallas kernels  168 us (96%)
  other arithmetic  3.78 us (2%)
  local copies, waits for them, and re-layouts  1.88 us (1%)
    pallas_call x1, Pallas kernels, body(): pl.pallas_call(kernel, out_shape=(jax.ShapeDtypeStruct((tok, width), BF16...  168 us

profile of v4, /device:TPU:1, one launch (start us, length us, event | category | flops | bytes accessed | tf_op | source)
XLA Modules:
  0.0 174.4 jit_solution(14192759375048338718)
XLA Ops:
  0.6 168.1 %moe_step.1 = (bf16[128,2048]{1,0:T(8,128)(2,1)}, bf16[2048,128]{1,0:T(8,128)(2,1)}, bf16[128,768]{1,0:T(8,128)(2,1)}) custom-call(bf16[128,2048]{1,0:T(8,128)(2,1)} %tokens.1, bf16[128,2048]{1,0:T(8,128)(2,1)} %cots.1, s32[8,128]{1,0:T(8,128)} %bitcast.18, f32[8,128]{1,0:T(8,128)} %bitcast.19, s32[8,128]{1,0:T(8,128)} %bitcast.20, s32[1,64]{1,0:T(1,128)} %bitcast.21, ...), custom_call_target="tpu_custom_call" | custom-call | flops 16000000000 | bytes 14680064 | tf_op jit(solution)/shard_map/moe_step/pallas_call | solution.py:585
  168.7 2.1 %bitcast_convert_fusion = f32[1,2048,128]{2,1,0:T(8,128)} fusion(bf16[2048,128]{1,0:T(8,128)(2,1)} %get-tuple-element.7), kind=kLoop, calls=%fused_computation | loop fusion | flops 262144 | bytes 1572864 | tf_op jit(solution)/shard_map/broadcast_in_dim | solution.py:654
  170.8 1.7 convert.3
  172.5 1.9 %copy.14 = bf16[128,2048]{1,0:T(8,128)(2,1)} copy(bf16[128,2048]{1,0:T(8,128)(2,1)} %get-tuple-element.12) | data formatting | bytes 1048576

commit v5 on v4

--- a/solution.py
+++ b/solution.py
@@ -507,22 +507,22 @@
     x_sum(0)
     ret_start(5)
     x_sum(1)
+    ret_start(6)
     rows_gone(0, 4)
     rows_gone(0, 3)
     rs_step(0, 3)
-    ret_start(6)
+    ret_start(7)
     z_back(0)
     z_back(1)
+    ret_start(8)
     rs_step(1, 3)
-    ret_start(7)
+    ret_start(9)
     dp_back(0)
     dp_back(1)
     rows_gone(0, 2)
     rows_gone(0, 1)
     rows_gone(0, 0)
     rs_step(0, 4)
-    ret_start(8)
-    ret_start(9)
     rs_step(1, 4)
     wait_bytes(yo.at[:, piece(0)], y_r.at[1, 0])
     turn(0, GP // BLK)

time: 175 us -> 175 us (level)
  no operation moved by 1% of the time
where the time goes in v5:
time: 175 us; the launch traced here: 174 us
  Pallas kernels  168 us (96%)
  other arithmetic  3.78 us (2%)
  local copies, waits for them, and re-layouts  1.88 us (1%)
    pallas_call x1, Pallas kernels, body(): pl.pallas_call(kernel, out_shape=(jax.ShapeDtypeStruct((tok, width), BF16...  168 us

profile of v5, /device:TPU:1, one launch (start us, length us, event | category | flops | bytes accessed | tf_op | source)
XLA Modules:
  0.0 174.4 jit_solution(4798744333452920308)
XLA Ops:
  0.6 168.1 %moe_step.1 = (bf16[128,2048]{1,0:T(8,128)(2,1)}, bf16[2048,128]{1,0:T(8,128)(2,1)}, bf16[128,768]{1,0:T(8,128)(2,1)}) custom-call(bf16[128,2048]{1,0:T(8,128)(2,1)} %tokens.1, bf16[128,2048]{1,0:T(8,128)(2,1)} %cots.1, s32[8,128]{1,0:T(8,128)} %bitcast.18, f32[8,128]{1,0:T(8,128)} %bitcast.19, s32[8,128]{1,0:T(8,128)} %bitcast.20, s32[1,64]{1,0:T(1,128)} %bitcast.21, ...), custom_call_target="tpu_custom_call" | custom-call | flops 16000000000 | bytes 14680064 | tf_op jit(solution)/shard_map/moe_step/pallas_call | solution.py:585
  168.7 2.1 %bitcast_convert_fusion = f32[1,2048,128]{2,1,0:T(8,128)} fusion(bf16[2048,128]{1,0:T(8,128)(2,1)} %get-tuple-element.7), kind=kLoop, calls=%fused_computation | loop fusion | flops 262144 | bytes 1572864 | tf_op jit(solution)/shard_map/broadcast_in_dim | solution.py:654
  170.8 1.7 convert.3
  172.5 1.9 %copy.14 = bf16[128,2048]{1,0:T(8,128)(2,1)} copy(bf16[128,2048]{1,0:T(8,128)(2,1)} %get-tuple-element.12) | data formatting | bytes 1048576
